TPU v7x, 256 devices: a whole 4x4x8 slice. The times are simulated.
256 devices in a mesh: pool: 32 (over y, x, core), tp: 8 (over z).
Axes of the slice: x: 4, y: 4, z: 8, core: 2. Of those that a mesh axis runs over, the one named last changes fastest.
Arguments:
- turn_query: bfloat16 [16384, 4096], P('pool', 'tp'), may hold values from -16 to 16
- turn_key: bfloat16 [16384, 1024], P('pool', 'tp'), may hold values from -16 to 16, as said below
- turn_value: bfloat16 [16384, 1024], P('pool', 'tp'), may hold values from -6 to 6
- pool_keys: bfloat16 [2048, 128, 1024], P('pool', None, 'tp'), may hold values from -16 to 16, as said below
- pool_values: bfloat16 [2048, 128, 1024], P('pool', None, 'tp'), may hold values from -6 to 6
- seat_session: int32 [64], replicated, may hold values from 0 to 63, as said below
- history_len: int32 [64], replicated, may hold values from 1 to 4096, as said below
- block_map: int32 [64, 32], replicated, may hold values from 0 to 2047, as said below
- out_weight: bfloat16 [4096, 8192], P('tp', 'pool'), may hold values from -0.1875 to 0.1875
Outputs:
- layer_out: bfloat16 [16384, 8192], P('pool', 'tp')
Inputs may be any that keep to these rules, and one draw needn't show every extreme that they name: `seat_session`: A permutation of the sessions. `history_len`: the sessions of one owner, chosen afresh in every draw, have length 4096. Every slot of the pool is named exactly once. Call block j of session s live when j * 128 < history_len[s]; the slot's pool index is block_map[s, j] // 64. The live blocks of one pool index that belong to the sessions of one owner number at most 2; some owner receives exactly 2 from every pool index. `turn_key`: Real-valued keys. `pool_keys`: Real-valued keys; slots not named by a live block hold values that are never read.
All inputs are finite; a program needn't handle non-finite values.
Results may differ from a plain program's by a relative error of at most 0.019.
Values may be sent and summed in bfloat16 or wider, within the bound.
No kernel may reach another device: no remote copies, remote signals or barrier semaphores. Data moves between devices by JAX's collectives and lax.ppermute only.
A program may use at most 128 MiB of HBM per device.

v0:
```python
import math

import jax
import jax.numpy as jnp
from jax import lax
from jax.sharding import PartitionSpec as P

rope_base = 1000000.0


def rotate(values, positions):
    half_dim = values.shape[-1] // 2
    freq_index = jnp.arange(half_dim, dtype=jnp.float32)
    inverse = rope_base ** (-2.0 * freq_index / values.shape[-1])
    angles = positions.astype(jnp.float32)[:, None, None] * inverse[None, None, :]
    cosine = jnp.cos(angles)
    sine_part = jnp.sin(angles)
    lower_half = values[..., :half_dim]
    upper_half = values[..., half_dim:]
    return jnp.concatenate(
        [
            lower_half * cosine - upper_half * sine_part,
            upper_half * cosine + lower_half * sine_part,
        ],
        axis=-1,
    )


def local(
    turn_query,
    turn_key,
    turn_value,
    pool_keys,
    pool_values,
    seat_session,
    history_len,
    block_map,
    out_weight,
):
    pooled_count = lax.axis_size("pool")
    current_index = lax.axis_index("pool")
    blocks_here = pool_keys.shape[0]
    rows_per_block = pool_keys.shape[1]
    head_dim = pool_keys.shape[2]
    block_count = block_map.shape[1]
    per_owner = seat_session.shape[0] // pooled_count
    capacity = per_owner * block_count // pooled_count
    element_count = per_owner * block_count
    turn_len = turn_query.shape[0] // per_owner
    group_size = turn_query.shape[1] // head_dim
    span_len = block_count * rows_per_block
    scaling = 1.0 / math.sqrt(head_dim)
    seat_length = history_len[seat_session]
    seat_map = block_map[seat_session]
    seats_per_device = (seat_map // blocks_here).reshape(pooled_count, element_count)
    seat_slot = (seat_map % blocks_here).reshape(pooled_count, element_count)
    block_numbers = jnp.arange(block_count, dtype=jnp.int32)
    alive_flags = (block_numbers[None, :] * rows_per_block < seat_length[:, None]).reshape(
        pooled_count, element_count
    )
    departing_rows = alive_flags & (seats_per_device == current_index)
    send_rank = jnp.cumsum(departing_rows.astype(jnp.int32), axis=1) - 1
    selected = departing_rows[:, None, :] & (
        send_rank[:, None, :] == jnp.arange(capacity, dtype=jnp.int32)[None, :, None]
    )
    slot_table = jnp.sum(jnp.where(selected, seat_slot[:, None, :], 0), axis=2).reshape(
        pooled_count * capacity
    )
    send_keys = pool_keys[slot_table]
    send_vals = pool_values[slot_table]
    own_lengths = lax.dynamic_slice_in_dim(seat_length, current_index * per_owner, per_owner, 0)
    token_ids = jnp.arange(turn_len, dtype=jnp.int32)
    causal = jnp.tile(token_ids[None, :] <= token_ids[:, None], (group_size, 1))

    def prepare_turn(seat_number):
        length = own_lengths[seat_number]
        row_lo = seat_number * turn_len
        turn_pos = length + token_ids
        queries = turn_query[row_lo : row_lo + turn_len].reshape(turn_len, group_size, head_dim)
        roped_query = rotate(queries.astype(jnp.float32), turn_pos).astype(jnp.bfloat16)
        roped_query = jnp.transpose(roped_query, (1, 0, 2)).reshape(group_size * turn_len, head_dim)
        new_keys = turn_key[row_lo : row_lo + turn_len].reshape(turn_len, 1, head_dim)
        roped_new = (
            rotate(new_keys.astype(jnp.float32), turn_pos)
            .astype(jnp.bfloat16)
            .reshape(turn_len, head_dim)
        )
        own_scores = (
            jnp.einsum("qd,kd->qk", roped_query, roped_new, preferred_element_type=jnp.float32)
            * scaling
        )
        own_scores = jnp.where(causal, own_scores, -jnp.inf)
        return (roped_query, own_scores)

    prepared = []
    arrived_keys, arrived_vals = (
        lax.all_to_all(send_keys, "pool", split_axis=0, concat_axis=0, tiled=True),
        lax.all_to_all(send_vals, "pool", split_axis=0, concat_axis=0, tiled=True),
    )
    prepared = [prepare_turn(seat_number) for seat_number in range(per_owner)]
    home_dev = lax.dynamic_slice_in_dim(seats_per_device, current_index, 1, 0)[0]
    resident_alive = lax.dynamic_slice_in_dim(alive_flags, current_index, 1, 0)[0]
    sources = jnp.arange(pooled_count, dtype=jnp.int32)[:, None]
    arriving = resident_alive[None, :] & (home_dev[None, :] == sources)
    rank_table = jnp.cumsum(arriving.astype(jnp.int32), axis=1) - 1
    arrive_rank = jnp.sum(jnp.where(arriving, rank_table, 0), axis=0)
    recv_index = jnp.where(resident_alive, home_dev * capacity + arrive_rank, 0)
    hist_keys = arrived_keys[recv_index].reshape(per_owner, span_len, head_dim)
    hist_vals = arrived_vals[recv_index].reshape(per_owner, span_len, head_dim)
    hist_pos = jnp.arange(span_len, dtype=jnp.int32)
    outputs = []
    for seat_number in range(per_owner):
        roped_query, own_scores = prepared[seat_number]
        length = own_lengths[seat_number]
        row_lo = seat_number * turn_len
        stored = hist_keys[seat_number].reshape(span_len, 1, head_dim)
        roped_hist = (
            rotate(stored.astype(jnp.float32), hist_pos)
            .astype(jnp.bfloat16)
            .reshape(span_len, head_dim)
        )
        far_scores = (
            jnp.einsum("qd,kd->qk", roped_query, roped_hist, preferred_element_type=jnp.float32)
            * scaling
        )
        far_scores = jnp.where((hist_pos < length)[None, :], far_scores, -jnp.inf)
        row_top = jnp.maximum(
            jnp.max(far_scores, axis=1, keepdims=True), jnp.max(own_scores, axis=1, keepdims=True)
        )
        far_weight = jnp.exp(far_scores - row_top)
        own_weight = jnp.exp(own_scores - row_top)
        denominator = jnp.sum(far_weight, axis=1, keepdims=True) + jnp.sum(
            own_weight, axis=1, keepdims=True
        )
        weighted = jnp.dot(
            far_weight.astype(jnp.bfloat16),
            hist_vals[seat_number],
            preferred_element_type=jnp.float32,
        )
        weighted = weighted + jnp.dot(
            own_weight.astype(jnp.bfloat16),
            turn_value[row_lo : row_lo + turn_len],
            preferred_element_type=jnp.float32,
        )
        head_rows = (
            (weighted / denominator).astype(jnp.bfloat16).reshape(group_size, turn_len, head_dim)
        )
        outputs.append(jnp.transpose(head_rows, (1, 0, 2)).reshape(turn_len, group_size * head_dim))
    attended = jnp.concatenate(outputs, axis=0)
    partial_value = jnp.dot(
        attended,
        lax.all_gather(out_weight, "pool", axis=1, tiled=True),
        preferred_element_type=jnp.float32,
    )
    partial_value = partial_value.astype(jnp.bfloat16).astype(jnp.float32)
    summed = lax.psum_scatter(
        partial_value.astype(jnp.bfloat16), "tp", scatter_dimension=1, tiled=True
    )
    return summed


def solution(mesh):
    return jax.shard_map(
        local,
        mesh=mesh,
        in_specs=(
            P("pool", "tp"),
            P("pool", "tp"),
            P("pool", "tp"),
            P("pool", None, "tp"),
            P("pool", None, "tp"),
            P(),
            P(),
            P(),
            P("tp", "pool"),
        ),
        out_specs=P("pool", "tp"),
        check_vma=False,
    )
```

profile of v0, /device:TPU:2, one launch (start us, length us, event | category | flops | bytes accessed | tf_op | source)
XLA Modules:
  0.0 230.9 jit_solution(12896060103432272524)
XLA Ops:
  6.5 0.7 all-gather.2.cloned.1.call-update
  7.3 0.8 copy.23
  8.1 0.7 compare_select_fusion.2
  8.7 0.6 gather_fusion.1
  9.3 0.1 gather.22
  9.4 1.4 gather_fusion
  10.8 0.1 lt.96
  10.9 0.1 lt.97
  11.0 0.1 lt.98
  11.1 0.1 lt.94
  11.3 0.2 reduce_window_sum.17
  11.5 0.1 select_reduce_fusion
  11.6 0.1 copy.24
  11.7 0.1 reshape.695
  11.9 2.1 gather_fusion.2
  14.0 7.6 %all-to-all-start = ((bf16[64,128,128]{2,1,0:T(8,128)(2,1)}), bf16[64,128,128]{2,1,0:T(8,128)(2,1)S(1)}, u32[]{:S(2)}, u32[]{:S(2)}) async-start(bf16[64,128,128]{2,1,0:T(8,128)(2,1)} %gather_fusion.2), calls=%async_computation | async-start | bytes 4194304 | tf_op jit(solution)/shard_map/all_to_all | solution.py:97
  21.7 0.1 dynamic_slice.9
  21.8 0.1 copy.29
  22.0 0.1 copy.30
  22.3 0.6 fusion.107
  22.9 0.6 add_convert_fusion.2
  23.5 0.6 add_convert_fusion.3
  24.2 0.5 multiply_cosine_fusion.4
  24.8 0.2 subtract_convert_fusion
  25.0 0.2 reduce_window_sum.18
  25.2 0.2 copy.22
  25.5 0.2 tile.13
  25.7 0.1 copy.31
  25.9 4.0 %gather_fusion.4 = bf16[64,128,128]{2,1,0:T(8,128)(2,1)} fusion(bf16[64,128,128]{2,1,0:T(8,128)(2,1)} %param.13, s32[1024]{0:T(1024)} %copy-done.14), kind=kCustom, calls=%fused_computation.4 | custom fusion | bytes 4194560 | tf_op jit(solution)/shard_map/gather | solution.py:70
  29.8 0.2 copy.27
  30.0 0.6 iota_compare_fusion.4
  30.7 0.6 iota_compare_fusion.2
  31.3 0.7 fusion.91
  32.0 0.6 iota_convert_fusion
  32.7 1.2 fusion.82
  33.9 1.9 fusion.109
  35.8 1.4 fusion.108
  37.3 16.0 %all-to-all-done = bf16[64,128,128]{2,1,0:T(8,128)(2,1)S(1)} async-done(((bf16[64,128,128]{2,1,0:T(8,128)(2,1)}), bf16[64,128,128]{2,1,0:T(8,128)(2,1)S(1)}, u32[]{:S(2)}, u32[]{:S(2)}) %all-to-all-start) | async-done | bytes 2097184 | tf_op jit(solution)/shard_map/all_to_all | solution.py:97
  53.3 6.0 %all-to-all-start.1 = ((bf16[64,128,128]{2,1,0:T(8,128)(2,1)}), bf16[64,128,128]{2,1,0:T(8,128)(2,1)}, u32[]{:S(2)}, u32[]{:S(2)}) async-start(bf16[64,128,128]{2,1,0:T(8,128)(2,1)} %gather_fusion.4), calls=%async_computation.1 | async-start | bytes 4194304 | tf_op jit(solution)/shard_map/all_to_all | solution.py:98
  59.3 0.2 reduce-scatter.2.cloned.1.call-start
  59.6 2.1 gather_fusion.3
  61.7 1.7 fusion.104
  63.4 0.2 bitcast_convert_fusion
  63.6 0.2 bitcast_convert_fusion.1
  63.8 0.3 copy-done.12
  64.1 11.0 %fusion.45 = (bf16[4096,64]{1,0:T(8,128)(2,1)S(1)}, bf16[4096,64]{1,0:T(8,128)(2,1)S(1)}, bf16[4096,64]{1,0:T(8,128)(2,1)S(1)}, bf16[4096,64]{1,0:T(8,128)(2,1)}) fusion(f32[4096,1,128]{2,0,1:T(8,128)S(1)} %bitcast_convert_fusion.1, f32[64]{0:T(128)S(1)} %copy-done.18, f32[4096]{0:T(1024)S(1)} %copy-done.12, f32[4096,1,128]{2,0,1:T(8,128)S(1)} %bitcast_convert_fusion), kind=kLoop, calls=%fused_computation.64 | loop fusion | flops 4456448 | bytes 6308096 | tf_op jit(solution)/shard_map/concatenate | solution.py:20
  75.1 3.0 %fusion = (f32[1024]{0:T(1024)S(1)}, f32[1024,4096]{1,0:T(8,128)S(1)}) fusion(pred[4096]{0:T(1024)(128)(4,1)S(1)} %iota_compare_fusion.4, bf16[1024,128]{1,0:T(8,128)(2,1)S(1)} %bitcast.88, bf16[4096,64]{1,0:T(8,128)(2,1)S(1)} %get-tuple-element.10, bf16[4096,64]{1,0:T(8,128)(2,1)S(1)} %get-tuple-element.9), kind=kOutput, calls=%fused_computation.10 | convolution fusion | flops 1088420864 | bytes 18096128 | tf_op jit(solution)/shard_map/qd,kd->qk/dot_general | solution.py:123
  78.1 0.2 fusion.46
  78.3 4.3 %fusion.2 = f32[1024]{0:T(1024)S(1)} fusion(f32[1024,4096]{1,0:T(8,128)S(1)} %get-tuple-element.46, f32[1024]{0:T(1024)S(1)} %max.16, pred[4096]{0:T(1024)(128)(4,1)S(1)} %iota_compare_fusion.4), kind=kLoop, calls=%fused_computation.12 | loop fusion | flops 16776192 | bytes 16789504 | tf_op jit(solution)/shard_map/reduce_sum | solution.py:132
  82.6 1.2 copy-done.2
  83.8 9.1 %all-to-all-done.1 = bf16[64,128,128]{2,1,0:T(8,128)(2,1)} async-done(((bf16[64,128,128]{2,1,0:T(8,128)(2,1)}), bf16[64,128,128]{2,1,0:T(8,128)(2,1)}, u32[]{:S(2)}, u32[]{:S(2)}) %all-to-all-start.1) | async-done | bytes 2097184 | tf_op jit(solution)/shard_map/all_to_all | solution.py:98
  92.9 2.6 %gather_fusion.5 = bf16[64,128,128]{2,1,0:T(8,128)(2,1)S(1)} fusion(bf16[64,128,128]{2,1,0:T(8,128)(2,1)} %all-to-all-done.1, s32[1024]{0:T(1024)S(1)} %pad_clamp_fusion), kind=kCustom, calls=%fused_computation.5 | custom fusion | bytes 4194560 | tf_op jit(solution)/shard_map/gather | solution.py:109
  95.5 1.2 fusion.105
  96.7 8.4 %fusion.8 = f32[1024,128]{1,0:T(8,128)S(1)} fusion(bf16[4096,128]{1,0:T(8,128)(2,1)S(1)} %bitcast.95, f32[1024,4096]{1,0:T(8,128)} %copy-done.2, f32[1024]{0:T(1024)S(1)} %max.16, pred[4096]{0:T(1024)(128)(4,1)S(1)} %iota_compare_fusion.4), kind=kOutput, calls=%fused_computation.18 | convolution fusion | flops 1090519040 | bytes 18358272 | tf_op jit(solution)/shard_map/dot_general | solution.py:135
  105.1 1.1 fusion.32
  106.1 1.1 copy.25
  107.3 2.9 %fusion.1 = (f32[1024]{0:T(1024)S(1)}, f32[1024,4096]{1,0:T(8,128)S(1)}) fusion(pred[4096]{0:T(1024)(128)(4,1)S(1)} %iota_compare_fusion.2, bf16[1024,128]{1,0:T(8,128)(2,1)S(1)} %bitcast.86, bf16[4096,64]{1,0:T(8,128)(2,1)S(1)} %get-tuple-element.29, bf16[4096,64]{1,0:T(8,128)(2,1)S(1)} %copy-done.3), kind=kOutput, calls=%fused_computation.11 | convolution fusion | flops 1088420864 | bytes 18096128 | tf_op jit(solution)/shard_map/qd,kd->qk/dot_general | solution.py:123
  110.3 0.2 fusion.48
  110.5 4.5 %fusion.4 = f32[1024]{0:T(1024)S(1)} fusion(f32[1024,4096]{1,0:T(8,128)S(1)} %get-tuple-element.42, f32[1024]{0:T(1024)S(1)} %max.17, pred[4096]{0:T(1024)(128)(4,1)S(1)} %iota_compare_fusion.2), kind=kLoop, calls=%fused_computation.14 | loop fusion | flops 16776192 | bytes 16789504 | tf_op jit(solution)/shard_map/reduce_sum | solution.py:132
  115.0 3.3 %fusion.6 = f32[1024,128]{1,0:T(8,128)S(1)} fusion(bf16[4096,128]{1,0:T(8,128)(2,1)S(1)} %bitcast.94, f32[1024,4096]{1,0:T(8,128)S(1)} %get-tuple-element.42, f32[1024]{0:T(1024)S(1)} %max.17, pred[4096]{0:T(1024)(128)(4,1)S(1)} %iota_compare_fusion.2), kind=kOutput, calls=%fused_computation.17 | convolution fusion | flops 1090519040 | bytes 18358272 | tf_op jit(solution)/shard_map/dot_general | solution.py:135
  118.3 0.4 fusion.33
  118.7 0.1 copy.28
  118.9 10.2 %convolution_convert_fusion = bf16[512,8192]{1,0:T(8,128)(2,1)} fusion(bf16[512,8192]{1,0:T(8,128)(2,1)} %all-gather.2.cloned.1.call-done, bf16[256,512]{0,1:T(8,128)(2,1)S(1)} %bitcast.90, bf16[256,512]{0,1:T(8,128)(2,1)S(1)} %bitcast.89), kind=kOutput, calls=%fused_computation.16 | convolution fusion | flops 4300210176 | bytes 17301504 | tf_op jit(solution)/shard_map/dot_general | solution.py:150
  129.1 95.0 %reduce-scatter.2.cloned.1.call-done = bf16[512,1024]{1,0:T(8,128)(2,1)} async-done(((bf16[512,8192]{1,0:T(8,128)(2,1)}), bf16[512,1024]{1,0:T(8,128)(2,1)}) %reduce-scatter.2.cloned.1.call-update) | async-done | bytes 1048592 | tf_op jit(solution)/shard_map/reduce_scatter | solution.py:156
  (85 shorter events, 0.5 us)
Async XLA Ops:
  6.5 5.3 %copy-start = (bf16[64,128,128]{2,1,0:T(8,128)(2,1)S(1)}, bf16[64,128,128]{2,1,0:T(8,128)(2,1)}, u32[]{:S(2)}) copy-start(bf16[64,128,128]{2,1,0:T(8,128)(2,1)} %param.12) | copy-start | bytes 6291460
  6.5 112.4 %all-gather.2.cloned.1.call-start = ((), (), s32[]{:S(2)}) async-start(), calls=%async_computation.3 | async-start | bytes 8650752 | tf_op jit(solution)/shard_map/all_gather | solution.py:152
  11.3 10.9 %copy-start.15 = (pred[32,64]{1,0:T(8,128)(4,1)}, pred[32,64]{1,0:T(8,128)(4,1)S(1)}, u32[]{:S(2)}) copy-start(pred[32,64]{1,0:T(8,128)(4,1)S(1)} %get-tuple-element.8) | copy-start | bytes 6148
  11.3 11.0 %copy-start.13 = (s32[32,64]{1,0:T(8,128)}, s32[32,64]{1,0:T(8,128)S(1)}, u32[]{:S(2)}) copy-start(s32[32,64]{1,0:T(8,128)S(1)} %get-tuple-element.7) | copy-start | bytes 24580
  11.9 2.2 copy-start.14
  11.9 9.9 %copy-start.10 = (bf16[512,512]{1,0:T(8,128)(2,1)S(1)}, bf16[512,512]{1,0:T(8,128)(2,1)}, u32[]{:S(2)}) copy-start(bf16[512,512]{1,0:T(8,128)(2,1)} %param.9) | copy-start | bytes 1572868
  14.0 39.3 %all-to-all-start = ((bf16[64,128,128]{2,1,0:T(8,128)(2,1)}), bf16[64,128,128]{2,1,0:T(8,128)(2,1)S(1)}, u32[]{:S(2)}, u32[]{:S(2)}) async-start(bf16[64,128,128]{2,1,0:T(8,128)(2,1)} %gather_fusion.2), calls=%async_computation | async-start | bytes 4194304 | tf_op jit(solution)/shard_map/all_to_all | solution.py:97
  22.2 2.6 %copy-start.16 = (f32[64]{0:T(128)}, f32[64]{0:T(128)S(1)}, u32[]{:S(2)}) copy-start(f32[64]{0:T(128)S(1)} %multiply_power_fusion) | copy-start | bytes 772
  22.2 2.5 %copy-start.24 = (pred[64]{0:T(512)(128)(4,1)}, pred[64]{0:T(512)(128)(4,1)S(1)}, u32[]{:S(2)}) copy-start(pred[64]{0:T(512)(128)(4,1)S(1)} %fusion.92) | copy-start | bytes 196
  22.3 2.5 %copy-start.26 = (s32[64]{0:T(128)}, s32[64]{0:T(128)S(1)}, u32[]{:S(2)}) copy-start(s32[64]{0:T(128)S(1)} %fusion.93) | copy-start | bytes 772
  23.5 1.2 copy-start.19
  24.2 0.6 copy-start.21
  24.8 7.9 %copy-start.11 = (bf16[512,128]{1,0:T(8,128)(2,1)S(1)}, bf16[512,128]{1,0:T(8,128)(2,1)}, u32[]{:S(2)}) copy-start(bf16[512,128]{1,0:T(8,128)(2,1)} %param.10) | copy-start | bytes 393220
  24.9 6.4 %copy-start.25 = (pred[64]{0:T(512)(128)(4,1)S(1)}, pred[64]{0:T(512)(128)(4,1)}, u32[]{:S(2)}) copy-start(pred[64]{0:T(512)(128)(4,1)} %copy-done.24) | copy-start | bytes 196
  25.0 6.4 %copy-start.27 = (s32[64]{0:T(128)S(1)}, s32[64]{0:T(128)}, u32[]{:S(2)}) copy-start(s32[64]{0:T(128)} %copy-done.26) | copy-start | bytes 772
  25.0 7.7 %copy-start.17 = (f32[64]{0:T(128)S(1)}, f32[64]{0:T(128)}, u32[]{:S(2)}) copy-start(f32[64]{0:T(128)} %copy-done.16) | copy-start | bytes 772
  25.0 7.7 %copy-start.20 = (f32[256]{0:T(256)S(1)}, f32[256]{0:T(256)}, u32[]{:S(2)}) copy-start(f32[256]{0:T(256)} %copy-done.19) | copy-start | bytes 3076
  25.0 7.7 %copy-start.22 = (f32[256]{0:T(256)S(1)}, f32[256]{0:T(256)}, u32[]{:S(2)}) copy-start(f32[256]{0:T(256)} %copy-done.21) | copy-start | bytes 3076
  25.4 10.4 %copy-start.4 = (bf16[4,256,128]{2,1,0:T(8,128)(2,1)}, bf16[4,256,128]{2,1,0:T(8,128)(2,1)S(1)}, u32[]{:S(2)}) copy-start(bf16[4,256,128]{2,1,0:T(8,128)(2,1)S(1)} %copy.22) | copy-start | bytes 786436
  53.3 39.6 %all-to-all-start.1 = ((bf16[64,128,128]{2,1,0:T(8,128)(2,1)}), bf16[64,128,128]{2,1,0:T(8,128)(2,1)}, u32[]{:S(2)}, u32[]{:S(2)}) async-start(bf16[64,128,128]{2,1,0:T(8,128)(2,1)} %gather_fusion.4), calls=%async_computation.1 | async-start | bytes 4194304 | tf_op jit(solution)/shard_map/all_to_all | solution.py:98
  59.3 164.8 %reduce-scatter.2.cloned.1.call-start = ((), (), s32[]{:S(2)}) async-start(), calls=%async_computation.4 | async-start | bytes 9437184 | tf_op jit(solution)/shard_map/reduce_scatter | solution.py:156
  63.4 0.7 copy-start.12
  63.4 0.7 copy-start.18
  64.1 11.0 %copy-start.5 = (bf16[4,256,128]{2,1,0:T(8,128)(2,1)S(1)}, bf16[4,256,128]{2,1,0:T(8,128)(2,1)}, u32[]{:S(2)}) copy-start(bf16[4,256,128]{2,1,0:T(8,128)(2,1)} %copy-done.4) | copy-start | bytes 786436
  75.1 3.0 %copy-start.23 = (f32[1024]{0:T(1024)S(1)}, f32[1024]{0:T(1024)}, u32[]{:S(2)}) copy-start(f32[1024]{0:T(1024)} %get-tuple-element.47) | copy-start | bytes 12292
  75.1 3.0 %copy-start.7 = (f32[1024,256]{0,1:T(8,128)S(1)}, f32[1024,256]{0,1:T(8,128)}, u32[]{:S(2)}) copy-start(f32[1024,256]{0,1:T(8,128)} %get-tuple-element.48) | copy-start | bytes 3145732
  78.1 5.7 %copy-start.2 = (f32[1024,4096]{1,0:T(8,128)}, f32[1024,4096]{1,0:T(8,128)S(1)}, u32[]{:S(2)}) copy-start(f32[1024,4096]{1,0:T(8,128)S(1)} %get-tuple-element.46) | copy-start | bytes 50331652
  96.7 8.4 %copy-start.8 = (f32[1024,256]{0,1:T(8,128)S(1)}, f32[1024,256]{0,1:T(8,128)}, u32[]{:S(2)}) copy-start(f32[1024,256]{0,1:T(8,128)} %get-tuple-element.48) | copy-start | bytes 3145732
  96.7 8.4 %copy-start.28 = (bf16[512,128]{1,0:T(8,128)(2,1)S(1)}, bf16[512,128]{1,0:T(8,128)(2,1)}, u32[]{:S(2)}) copy-start(bf16[512,128]{1,0:T(8,128)(2,1)} %param.11) | copy-start | bytes 393220
  96.7 10.6 %copy-start.3 = (bf16[4096,64]{1,0:T(8,128)(2,1)S(1)}, bf16[4096,64]{1,0:T(8,128)(2,1)}, u32[]{:S(2)}) copy-start(bf16[4096,64]{1,0:T(8,128)(2,1)} %get-tuple-element.30) | copy-start | bytes 1572868
  107.3 3.0 %copy-start.6 = (f32[1024,256]{0,1:T(8,128)S(1)}, f32[1024,256]{0,1:T(8,128)}, u32[]{:S(2)}) copy-start(f32[1024,256]{0,1:T(8,128)} %get-tuple-element.44) | copy-start | bytes 3145732
  110.5 4.6 %copy-start.9 = (bf16[32,128,128]{2,1,0:T(8,128)(2,1)S(1)}, bf16[32,128,128]{2,1,0:T(8,128)(2,1)}, u32[]{:S(2)}) copy-start(bf16[32,128,128]{2,1,0:T(8,128)(2,1)} %get-tuple-element.16) | copy-start | bytes 3145732
  115.0 3.3 %copy-start.29 = (bf16[512,128]{1,0:T(8,128)(2,1)S(1)}, bf16[512,128]{1,0:T(8,128)(2,1)}, u32[]{:S(2)}) copy-start(bf16[512,128]{1,0:T(8,128)(2,1)} %param.11) | copy-start | bytes 393220
  129.1 95.0 %copy-start.1 = (bf16[64,128,128]{2,1,0:T(8,128)(2,1)S(1)}, bf16[64,128,128]{2,1,0:T(8,128)(2,1)}, u32[]{:S(2)}) copy-start(bf16[64,128,128]{2,1,0:T(8,128)(2,1)} %param.12) | copy-start | bytes 6291460
Sparse Core Ops, SparseCore 0:
  9.8 99.1 all-gather.1
  129.3 94.8 reduce-scatter.1
where the time goes:
time: 232 us; the launch traced here: 231 us
  waiting for transfers between devices  121 us (52%)
  matrix products  32.6 us (14%)
  other arithmetic  27.8 us (12%)
  local copies, waits for them, and re-layouts  21.7 us (9%)
  between operations  14.1 us (6%)
  starting transfers between devices  13.9 us (6%)
    reduce_scatter x1, waiting for transfers between devices, local(): lax.psum_scatter(partial_value.astype(jnp.bfloat16), 'tp', scatter_dimens...  95 us
    all_to_all x1, waiting for transfers between devices, local(): lax.all_to_all(send_keys, 'pool', split_axis=0, concat_axis=0, tiled=True)  16 us
    concatenate x2, other arithmetic, rotate(): jnp.concatenate([lower_half * cosine - upper_half * sine_part, upper_half...  12.2 us
    dot_general x2, matrix products, local(): jnp.dot(far_weight.astype(jnp.bfloat16), hist_vals[seat_number], preferre...  11.7 us
    dot_general x1, matrix products, local(): jnp.dot(attended, lax.all_gather(out_weight, 'pool', axis=1, tiled=True),...  10.2 us
    all_to_all x1, waiting for transfers between devices, local(): lax.all_to_all(send_vals, 'pool', split_axis=0, concat_axis=0, tiled=True)  9.08 us
    reduce_sum x2, other arithmetic, local(): jnp.sum(far_weight, axis=1, keepdims=True)  8.82 us
    all_to_all x1, starting transfers between devices, local(): lax.all_to_all(send_keys, 'pool', split_axis=0, concat_axis=0, tiled=True)  7.62 us
  transfers between devices with their start and end apart: 4, of which 3 were waited for; matrix products, arithmetic and copies ran while one was open for 30% of the time, Pallas kernels for 0%

commit v1 on v0

v1 whole, which is shorter than its diff:
```python
import functools
import math

import jax
import jax.numpy as jnp
from jax import lax
from jax.experimental import pallas as pl
from jax.experimental.pallas import tpu as pltpu
from jax.sharding import PartitionSpec as P

rope_base = 1000000.0
CHUNK_BLOCKS = 8


def inverse_frequencies(head_dim):
    half_dim = head_dim // 2
    freq_index = jnp.arange(half_dim, dtype=jnp.float32)
    return rope_base ** (-2.0 * freq_index / head_dim)


def angle_tables(positions, head_dim):
    angles = positions.astype(jnp.float32)[:, None] * inverse_frequencies(head_dim)[None, :]
    cosine, sine = jnp.cos(angles), jnp.sin(angles)
    return jnp.concatenate([cosine, cosine], axis=1), jnp.concatenate([-sine, sine], axis=1)


def rotate_halves(values):
    half_dim = values.shape[-1] // 2
    return jnp.concatenate([values[..., half_dim:], values[..., :half_dim]], axis=-1)


def send_kernel(slot_ref, keys_ref, vals_ref, out_ref, sem):
    count = out_ref.shape[0]

    @pl.loop(0, count)
    def _(i):
        slot = slot_ref[i]
        pltpu.make_async_copy(keys_ref.at[slot], out_ref.at[i, 0], sem.at[0]).start()
        pltpu.make_async_copy(vals_ref.at[slot], out_ref.at[i, 1], sem.at[0]).start()

    pltpu.make_async_copy(out_ref, out_ref, sem.at[0]).wait()


def gather_send(slot_table, pool_keys, pool_values):
    count = slot_table.shape[0]
    return pl.pallas_call(
        send_kernel,
        out_shape=jax.ShapeDtypeStruct((count, 2) + pool_keys.shape[1:], pool_keys.dtype),
        grid_spec=pltpu.PrefetchScalarGridSpec(
            num_scalar_prefetch=1,
            grid=(1,),
            in_specs=[pl.BlockSpec(memory_space=pl.ANY)] * 2,
            out_specs=pl.BlockSpec(memory_space=pl.ANY),
            scratch_shapes=[pltpu.SemaphoreType.DMA((1,))],
        ),
    )(slot_table, pool_keys, pool_values)


def attention_kernel(
    seat,
    index_ref,
    length_ref,
    query_ref,
    turn_key_ref,
    turn_val_ref,
    row_cos_ref,
    row_sin_ref,
    base_cos_ref,
    base_sin_ref,
    arrived_ref,
    out_ref,
    blocks,
    roped,
    top_ref,
    total_ref,
    acc_ref,
    sems,
):
    heads, turn_len, head_dim = query_ref.shape
    block_count, _, block_rows, _ = blocks.shape
    chunk_rows = CHUNK_BLOCKS * block_rows
    scaling = math.log2(math.e) / math.sqrt(head_dim)
    length = length_ref[seat]
    chunks = pl.cdiv(length, chunk_rows)
    full = length // chunk_rows

    def copy(j):
        return pltpu.make_async_copy(
            arrived_ref.at[index_ref[seat * block_count + j]], blocks.at[j], sems.at[j]
        )

    @pl.loop(0, chunks * CHUNK_BLOCKS)
    def _(j):
        copy(j).start()

    def scores(h, keys):
        return lax.dot_general(
            query_ref[h], keys, (((1,), (1,)), ((), ())), preferred_element_type=jnp.float32
        )

    rows = lax.broadcasted_iota(jnp.int32, (turn_len, turn_len), 0)
    cols = lax.broadcasted_iota(jnp.int32, (turn_len, turn_len), 1)
    for h in range(heads):
        s = jnp.where(cols <= rows, scores(h, turn_key_ref[...]), -jnp.inf)
        top = jnp.max(s, axis=1, keepdims=True)
        weight = jnp.exp2((s - top) * scaling)
        top_ref[h] = top
        total_ref[h] = jnp.sum(weight, axis=1, keepdims=True)
        acc_ref[h] = jnp.dot(
            weight.astype(jnp.bfloat16), turn_val_ref[...], preferred_element_type=jnp.float32
        )

    def chunk_step(c, masked):
        for i in range(CHUNK_BLOCKS):
            j = c * CHUNK_BLOCKS + i
            copy(j).wait()
            base_cos = base_cos_ref[pl.ds(j, 1), :]
            base_sin = base_sin_ref[pl.ds(j, 1), :]
            row_cos, row_sin = row_cos_ref[...], row_sin_ref[...]
            cosine = row_cos * base_cos - row_sin * base_sin
            sine = row_sin * base_cos + row_cos * base_sin
            key = blocks[j, 0].astype(jnp.float32)
            key = key * cosine + pltpu.roll(key, head_dim // 2, 1) * sine
            roped[i * block_rows : (i + 1) * block_rows, :] = key.astype(jnp.bfloat16)
        vals = blocks[pl.ds(c * CHUNK_BLOCKS, CHUNK_BLOCKS), 1].reshape(chunk_rows, head_dim)
        keys = roped[...]
        for h in range(heads):
            s = scores(h, keys)
            if masked:
                place = c * chunk_rows + lax.broadcasted_iota(jnp.int32, s.shape, 1)
                s = jnp.where(place < length, s, -jnp.inf)
            old = top_ref[h]
            top = jnp.maximum(old, jnp.max(s, axis=1, keepdims=True))
            weight = jnp.exp2((s - top) * scaling)
            fade = jnp.exp2((old - top) * scaling)
            top_ref[h] = top
            total_ref[h] = total_ref[h] * fade + jnp.sum(weight, axis=1, keepdims=True)
            acc_ref[h] = acc_ref[h] * fade + jnp.dot(
                weight.astype(jnp.bfloat16), vals, preferred_element_type=jnp.float32
            )

    @pl.loop(0, full)
    def _(c):
        chunk_step(c, False)

    @pl.when(full < chunks)
    def _():
        chunk_step(full, True)

    for h in range(heads):
        out_ref[:, h * head_dim : (h + 1) * head_dim] = (acc_ref[h] / total_ref[h]).astype(
            jnp.bfloat16
        )


def attend(seat, recv_index, lengths, query, turn_key, turn_val, tables, arrived):
    heads, turn_len, head_dim = query.shape
    block_rows = arrived.shape[2]
    block_count = recv_index.shape[0] // lengths.shape[0]
    vmem = pl.BlockSpec(memory_space=pltpu.VMEM)
    return pl.pallas_call(
        functools.partial(attention_kernel, seat),
        out_shape=jax.ShapeDtypeStruct((turn_len, heads * head_dim), jnp.bfloat16),
        grid_spec=pltpu.PrefetchScalarGridSpec(
            num_scalar_prefetch=2,
            grid=(1,),
            in_specs=[vmem] * 7 + [pl.BlockSpec(memory_space=pl.ANY)],
            out_specs=vmem,
            scratch_shapes=[
                pltpu.VMEM((block_count, 2, block_rows, head_dim), jnp.bfloat16),
                pltpu.VMEM((CHUNK_BLOCKS * block_rows, head_dim), jnp.bfloat16),
                pltpu.VMEM((heads, turn_len, 1), jnp.float32),
                pltpu.VMEM((heads, turn_len, 1), jnp.float32),
                pltpu.VMEM((heads, turn_len, head_dim), jnp.float32),
                pltpu.SemaphoreType.DMA((block_count,)),
            ],
        ),
        compiler_params=pltpu.CompilerParams(vmem_limit_bytes=40 * 1024 * 1024),
        cost_estimate=pl.CostEstimate(
            flops=4 * heads * turn_len * (block_count * block_rows + turn_len) * head_dim,
            bytes_accessed=2 * 1024 * 1024,
            transcendentals=heads * turn_len * (block_count * block_rows + turn_len),
        ),
    )(recv_index, lengths, query, turn_key, turn_val, *tables, arrived)


def project_kernel(order_ref, rows_ref, weight_ref, out_ref, acc_ref):
    step = pl.program_id(0)
    pieces, _, width = weight_ref.shape
    for j in range(pieces):
        part = jnp.dot(rows_ref[0], weight_ref[j], preferred_element_type=jnp.float32)
        cols = slice(j * width, (j + 1) * width)

        @pl.when(step == 0)
        def _():
            acc_ref[:, cols] = part

        @pl.when(step > 0)
        def _():
            acc_ref[:, cols] += part

    @pl.when(step == pl.num_programs(0) - 1)
    def _():
        out_ref[...] = acc_ref[...].astype(jnp.bfloat16)


def project(order, gathered, weights):
    groups, rows, depth = gathered.shape
    pieces = weights.shape[0] // groups
    width = weights.shape[2]
    return pl.pallas_call(
        project_kernel,
        out_shape=jax.ShapeDtypeStruct((rows, pieces * width), jnp.bfloat16),
        grid_spec=pltpu.PrefetchScalarGridSpec(
            num_scalar_prefetch=1,
            grid=(groups,),
            in_specs=[
                pl.BlockSpec((1, rows, depth), lambda u, order: (order[u], 0, 0)),
                pl.BlockSpec((pieces, depth, width), lambda u, order: (u, 0, 0)),
            ],
            out_specs=pl.BlockSpec((rows, pieces * width), lambda u, order: (0, 0)),
            scratch_shapes=[pltpu.VMEM((rows, pieces * width), jnp.float32)],
        ),
        compiler_params=pltpu.CompilerParams(vmem_limit_bytes=40 * 1024 * 1024),
    )(order, gathered, weights)


def local(
    turn_query,
    turn_key,
    turn_value,
    pool_keys,
    pool_values,
    seat_session,
    history_len,
    block_map,
    out_weight,
):
    pooled_count = lax.axis_size("pool")
    tp_count = lax.axis_size("tp")
    current_index = lax.axis_index("pool")
    tp_index = lax.axis_index("tp")
    blocks_here, rows_per_block, head_dim = pool_keys.shape
    block_count = block_map.shape[1]
    per_owner = seat_session.shape[0] // pooled_count
    capacity = per_owner * block_count // pooled_count
    element_count = per_owner * block_count
    turn_len = turn_query.shape[0] // per_owner
    group_size = turn_query.shape[1] // head_dim
    pieces = pooled_count // tp_count

    seat_length = history_len[seat_session]
    seat_map = block_map[seat_session]
    seats_per_device = (seat_map // blocks_here).reshape(pooled_count, element_count)
    seat_slot = (seat_map % blocks_here).reshape(pooled_count, element_count)
    block_numbers = jnp.arange(block_count, dtype=jnp.int32)
    alive_flags = (block_numbers[None, :] * rows_per_block < seat_length[:, None]).reshape(
        pooled_count, element_count
    )
    departing_rows = alive_flags & (seats_per_device == current_index)
    send_rank = jnp.cumsum(departing_rows.astype(jnp.int32), axis=1) - 1
    selected = departing_rows[:, None, :] & (
        send_rank[:, None, :] == jnp.arange(capacity, dtype=jnp.int32)[None, :, None]
    )
    slot_table = jnp.sum(jnp.where(selected, seat_slot[:, None, :], 0), axis=2).reshape(
        pooled_count * capacity
    )
    sent = gather_send(slot_table, pool_keys, pool_values)
    arrived = lax.all_to_all(sent, "pool", split_axis=0, concat_axis=0, tiled=True)

    moves = []
    for p in range(pooled_count):
        for t in range(tp_count):
            plane = p // pieces
            place = (plane ^ t) * pieces + p % pieces
            moves.append((p * tp_count + t, place * tp_count + plane))
    moved = lax.ppermute(out_weight, ("pool", "tp"), moves)
    weights = lax.all_gather(moved, "pool", axis=0, tiled=False)

    own_lengths = lax.dynamic_slice_in_dim(seat_length, current_index * per_owner, per_owner, 0)
    home_dev = lax.dynamic_slice_in_dim(seats_per_device, current_index, 1, 0)[0]
    resident_alive = lax.dynamic_slice_in_dim(alive_flags, current_index, 1, 0)[0]
    sources = jnp.arange(pooled_count, dtype=jnp.int32)[:, None]
    arriving = resident_alive[None, :] & (home_dev[None, :] == sources)
    rank_table = jnp.cumsum(arriving.astype(jnp.int32), axis=1) - 1
    arrive_rank = jnp.sum(jnp.where(arriving, rank_table, 0), axis=0)
    recv_index = jnp.where(resident_alive, home_dev * capacity + arrive_rank, 0)

    row_tables = angle_tables(jnp.arange(rows_per_block, dtype=jnp.int32), head_dim)
    base_tables = angle_tables(block_numbers * rows_per_block, head_dim)
    tables = (*row_tables, *base_tables)
    token_ids = jnp.arange(turn_len, dtype=jnp.int32)
    order = jnp.arange(tp_count, dtype=jnp.int32) ^ tp_index

    outputs = []
    for seat in range(per_owner):
        cosine, sine = angle_tables(own_lengths[seat] + token_ids, head_dim)
        rows = slice(seat * turn_len, (seat + 1) * turn_len)
        queries = turn_query[rows].astype(jnp.float32).reshape(turn_len, group_size, head_dim)
        queries = queries * cosine[:, None, :] + rotate_halves(queries) * sine[:, None, :]
        queries = jnp.transpose(queries.astype(jnp.bfloat16), (1, 0, 2))
        new_keys = turn_key[rows].astype(jnp.float32)
        new_keys = (new_keys * cosine + rotate_halves(new_keys) * sine).astype(jnp.bfloat16)
        attended = attend(
            seat, recv_index, own_lengths, queries, new_keys, turn_value[rows], tables, arrived
        )
        outputs.append(lax.all_gather(attended, "tp", axis=0, tiled=False))
    return jnp.concatenate([project(order, gathered, weights) for gathered in outputs], axis=0)


def solution(mesh):
    return jax.shard_map(
        local,
        mesh=mesh,
        in_specs=(
            P("pool", "tp"),
            P("pool", "tp"),
            P("pool", "tp"),
            P("pool", None, "tp"),
            P("pool", None, "tp"),
            P(),
            P(),
            P(),
            P("tp", "pool"),
        ),
        out_specs=P("pool", "tp"),
        check_vma=False,
    )
```

time: 232 us -> 388 us (1.67)
  Pallas kernels: 0 us -> 165 us
  waiting for transfers between devices: 121 us -> 178 us
  matrix products: 32.6 us -> 0 us
  other arithmetic: 27.8 us -> 6.1 us
  local copies, waits for them, and re-layouts: 21.7 us -> 15.9 us
  starting transfers between devices: 13.9 us -> 8.62 us
    pallas_call x0 -> x5, Pallas kernels: none -> 165 us  [the longest x1 129 us: gather_send(): pl.pallas_call(send_kernel, out_shape=jax.ShapeDtypeStruct((count, 2) + p...]
    all_gather x1 -> x3, waiting for transfers between devices: 0.02 us -> 132 us  [the longest x2 74.8 us: local(): outputs.append(lax.all_gather(attended, 'tp', axis=0, tiled=False))]
    reduce_scatter x1 -> x0, waiting for transfers between devices: 95 us -> none  [local(): lax.psum_scatter(partial_value.astype(jnp.bfloat16), 'tp', scatter_dimens...]
    dot_general x9 -> x0, matrix products: 32.6 us -> none  [the longest x2 11.7 us: local(): jnp.dot(far_weight.astype(jnp.bfloat16), hist_vals[seat_number], preferre...]
    all_to_all x2 -> x1, waiting for transfers between devices: 25.1 us -> 46 us  [local(): lax.all_to_all(sent, 'pool', split_axis=0, concat_axis=0, tiled=True)]
    concatenate x2 -> x3, other arithmetic: 12.2 us -> 1.22 us  [the longest x1 1.04 us: local(): jnp.concatenate([project(order, gathered, weights) for gathered in output...]
    gather x4 -> x0, local copies, waits for them, and re-layouts: 10.8 us -> none  [the longest x1 3.95 us: local(): send_vals = pool_values[slot_table]]
    reduce_sum x4 -> x0, other arithmetic: 9.17 us -> none  [the longest x2 8.82 us: local(): jnp.sum(far_weight, axis=1, keepdims=True)]
  transfers between devices with their start and end apart: 4 -> 5, of which waited for: 3 -> 4; matrix products, arithmetic and copies ran while one was open for 30% -> 2% of each run, Pallas kernels for 0% -> 4%
where the time goes in v1:
time: 388 us; the launch traced here: 387 us
  waiting for transfers between devices  178 us (46%)
  Pallas kernels  165 us (43%)
  local copies, waits for them, and re-layouts  15.9 us (4%)
  between operations  13.4 us (3%)
  starting transfers between devices  8.62 us (2%)
  other arithmetic  6.1 us (2%)
    pallas_call x1, Pallas kernels, gather_send(): pl.pallas_call(send_kernel, out_shape=jax.ShapeDtypeStruct((count, 2) + p...  129 us
    all_gather x2, waiting for transfers between devices, local(): outputs.append(lax.all_gather(attended, 'tp', axis=0, tiled=False))  74.8 us
    all_gather x1, waiting for transfers between devices, local(): weights = lax.all_gather(moved, 'pool', axis=0, tiled=False)  57.4 us
    all_to_all x1, waiting for transfers between devices, local(): lax.all_to_all(sent, 'pool', split_axis=0, concat_axis=0, tiled=True)  46 us
    pallas_call x2, Pallas kernels, project(): pl.pallas_call(project_kernel, out_shape=jax.ShapeDtypeStruct((rows, piec...  21.2 us
    pallas_call x2, Pallas kernels, attend(): pl.pallas_call(functools.partial(attention_kernel, seat), out_shape=jax.S...  15 us
    unnamed x23, local copies, waits for them, and re-layouts  11.7 us
    all_to_all x1, starting transfers between devices, local(): lax.all_to_all(sent, 'pool', split_axis=0, concat_axis=0, tiled=True)  7.82 us
  transfers between devices with their start and end apart: 5, of which 4 were waited for; matrix products, arithmetic and copies ran while one was open for 2% of the time, Pallas kernels for 4%

profile of v1, /device:TPU:2, one launch (start us, length us, event | category | flops | bytes accessed | tf_op | source)
XLA Modules:
  0.0 387.3 jit_solution(12264349853672487495)
XLA Ops:
  6.5 0.0 copy-start
  6.5 0.7 compare_select_fusion
  7.2 0.8 copy.20
  8.0 0.0 copy-done
  8.0 0.8 gather_fusion
  8.8 0.6 gather_fusion.1
  9.4 0.1 gather.10
  9.5 0.1 lt.51
  9.6 0.1 lt.52
  9.7 0.1 lt.53
  9.8 0.1 lt.48
  9.9 0.2 reduce_window_sum.18
  10.1 0.1 select_reduce_fusion
  10.2 0.1 copy.25
  10.3 0.6 reshape.182.slot_ref
  10.9 128.8 %shard_map.91 = bf16[64,2,128,128]{3,2,1,0:T(8,128)(2,1)} custom-call(s32[64]{0:T(128)} %reshape.182.slot_ref, bf16[64,128,128]{2,1,0:T(8,128)(2,1)} %keys_ref.1, bf16[64,128,128]{2,1,0:T(8,128)(2,1)} %vals_ref.1), custom_call_target="tpu_custom_call" | custom-call | tf_op jit(solution)/shard_map/pallas_call | solution.py:46
  139.8 0.0 copy-start.6
  139.8 7.8 %all-to-all-start = ((bf16[64,2,128,128]{3,2,1,0:T(8,128)(2,1)}), bf16[64,2,128,128]{3,2,1,0:T(8,128)(2,1)}, u32[]{:S(2)}, u32[]{:S(2)}) async-start(bf16[64,2,128,128]{3,2,1,0:T(8,128)(2,1)} %shard_map.91), calls=%async_computation | async-start | bytes 8388608 | tf_op jit(solution)/shard_map/all_to_all | solution.py:269
  147.6 0.0 copy-start.8
  147.6 0.0 copy-start.5
  147.6 0.0 all-gather.7.cloned.1.call-start
  147.7 0.1 dynamic_slice.11.length_ref
  147.8 0.0 copy-done.6
  147.8 0.1 copy.30
  148.0 0.1 copy.22
  148.2 0.2 reduce_window_sum.17
  148.4 0.6 fusion.27
  149.0 1.3 add_convert_fusion
  150.3 0.1 fusion.18
  150.5 0.1 pad_maximum_fusion.7
  150.6 0.3 fusion.13
  150.9 0.1 pad_maximum_fusion.5
  151.0 0.0 copy-done.8
  151.1 0.1 fusion.25
  151.2 1.0 fusion.10
  152.2 0.3 fusion.7
  152.5 0.2 fusion.21
  152.7 0.3 fusion.5.query_ref
  153.0 46.0 %all-to-all-done.arrived_ref = bf16[64,2,128,128]{3,2,1,0:T(8,128)(2,1)} async-done(((bf16[64,2,128,128]{3,2,1,0:T(8,128)(2,1)}), bf16[64,2,128,128]{3,2,1,0:T(8,128)(2,1)}, u32[]{:S(2)}, u32[]{:S(2)}) %all-to-all-start) | async-done | bytes 4194336 | tf_op jit(solution)/shard_map/all_to_all | solution.py:269
  199.0 9.0 %shard_map.92 = bf16[256,512]{1,0:T(8,128)(2,1)} custom-call(s32[64]{0:T(128)S(1)} %add_select_fusion.2.index_ref, s32[2]{0:T(128)S(1)} %dynamic_slice.11.length_ref, bf16[4,256,128]{2,1,0:T(8,128)(2,1)S(1)} %fusion.5.query_ref, bf16[256,128]{1,0:T(8,128)(2,1)S(1)} %get-tuple-element.5.turn_key_ref, bf16[256,128]{1,0:T(8,128)(2,1)S(1)} %get-tuple-element.19.turn_val_ref, ...), custom_call_target="tpu_custom_call" | custom-call | flops 2281701376 | bytes 2097152 | tf_op jit(solution)/shard_map/pallas_call | solution.py:161
  208.0 0.0 all-gather.7.cloned.1.call-update
  208.1 0.0 all-gather.9.cloned.1.call-start
  208.1 0.7 collective-permute-start
  208.8 0.0 collective-permute-done
  208.8 0.0 copy-start.7
  208.8 0.7 copy-done.7
  209.5 0.0 all-gather.9.cloned.1.call-update
  209.6 0.0 all-gather.11.cloned.1.call-start
  209.6 0.1 copy.31
  209.8 0.1 copy.27
  209.9 0.2 fusion.23
  210.1 0.3 fusion.4.query_ref
  210.4 6.0 %shard_map.94 = bf16[256,512]{1,0:T(8,128)(2,1)} custom-call(s32[64]{0:T(128)S(1)} %add_select_fusion.2.index_ref, s32[2]{0:T(128)S(1)} %dynamic_slice.11.length_ref, bf16[4,256,128]{2,1,0:T(8,128)(2,1)S(1)} %fusion.4.query_ref, bf16[256,128]{1,0:T(8,128)(2,1)S(1)} %get-tuple-element.22.turn_key_ref, bf16[256,128]{1,0:T(8,128)(2,1)S(1)} %get-tuple-element.20.turn_val_ref, ...), custom_call_target="tpu_custom_call" | custom-call | flops 2281701376 | bytes 2097152 | tf_op jit(solution)/shard_map/pallas_call | solution.py:161
  216.3 0.0 all-gather.11.cloned.1.call-update
  216.4 47.5 %all-gather.7.cloned.1.call-done = bf16[2048,512]{1,0:T(8,128)(2,1)} async-done(((bf16[256,512]{1,0:T(8,128)(2,1)}), bf16[2048,512]{1,0:T(8,128)(2,1)}) %all-gather.7.cloned.1.call-update) | async-done | bytes 2097168 | tf_op jit(solution)/shard_map/all_gather | solution.py:307
  263.9 57.4 %all-gather.9.cloned.1.call-done = bf16[16384,256]{1,0:T(8,128)(2,1)} async-done(((bf16[512,256]{1,0:T(8,128)(2,1)}), bf16[16384,256]{1,0:T(8,128)(2,1)}) %all-gather.9.cloned.1.call-update) | async-done | bytes 8388624 | tf_op jit(solution)/shard_map/all_gather | solution.py:278
  321.3 3.4 copy-done.1
  324.6 1.6 copy-done.3
  326.2 10.6 %shard_map.93 = bf16[256,1024]{1,0:T(8,128)(2,1)S(1)} custom-call(s32[8]{0:T(128)S(1)} %iota_xor_fusion.order_ref, bf16[8,256,512]{2,1,0:T(8,128)(2,1)S(1)} %bitcast.23, bf16[32,512,256]{2,1,0:T(8,128)(2,1)S(1)} %bitcast.21), custom_call_target="tpu_custom_call" | custom-call | tf_op jit(solution)/shard_map/pallas_call | solution.py:211
  336.8 27.3 %all-gather.11.cloned.1.call-done = bf16[2048,512]{1,0:T(8,128)(2,1)} async-done(((bf16[256,512]{1,0:T(8,128)(2,1)}), bf16[2048,512]{1,0:T(8,128)(2,1)}) %all-gather.11.cloned.1.call-update) | async-done | bytes 2097168 | tf_op jit(solution)/shard_map/all_gather | solution.py:307
  364.2 3.4 copy-done.2
  367.5 1.6 copy-done.4
  369.1 10.6 %shard_map.95 = bf16[256,1024]{1,0:T(8,128)(2,1)S(1)} custom-call(s32[8]{0:T(128)S(1)} %iota_xor_fusion.order_ref, bf16[8,256,512]{2,1,0:T(8,128)(2,1)S(1)} %bitcast.24, bf16[32,512,256]{2,1,0:T(8,128)(2,1)S(1)} %bitcast.22), custom_call_target="tpu_custom_call" | custom-call | tf_op jit(solution)/shard_map/pallas_call | solution.py:211
  379.7 1.0 pad_maximum_fusion
  (24 shorter events, 0.2 us)
Async XLA Ops:
  6.5 1.5 copy-start
  139.8 8.0 %copy-start.6 = (bf16[512,512]{1,0:T(8,128)(2,1)S(1)}, bf16[512,512]{1,0:T(8,128)(2,1)}, u32[]{:S(2)}) copy-start(bf16[512,512]{1,0:T(8,128)(2,1)} %param.9) | copy-start | bytes 1572868
  139.8 59.2 %all-to-all-start = ((bf16[64,2,128,128]{3,2,1,0:T(8,128)(2,1)}), bf16[64,2,128,128]{3,2,1,0:T(8,128)(2,1)}, u32[]{:S(2)}, u32[]{:S(2)}) async-start(bf16[64,2,128,128]{3,2,1,0:T(8,128)(2,1)} %shard_map.91), calls=%async_computation | async-start | bytes 8388608 | tf_op jit(solution)/shard_map/all_to_all | solution.py:269
  147.6 3.4 copy-start.8
  147.6 3.4 copy-start.5
  147.6 116.2 %all-gather.7.cloned.1.call-start = ((), (), s32[]{:S(2)}) async-start(), calls=%async_computation.1 | async-start | bytes 2359296 | tf_op jit(solution)/shard_map/all_gather | solution.py:307
  199.0 9.1 %copy-start.9 = (bf16[512,256]{1,0:T(8,128)(2,1)S(1)}, bf16[512,256]{1,0:T(8,128)(2,1)}, u32[]{:S(2)}) copy-start(bf16[512,256]{1,0:T(8,128)(2,1)} %param.17) | copy-start | bytes 786436
  208.1 113.2 %all-gather.9.cloned.1.call-start = ((), (), s32[]{:S(2)}) async-start(), calls=%async_computation.2 | async-start | bytes 8650752 | tf_op jit(solution)/shard_map/all_gather | solution.py:278
  208.1 0.7 collective-permute-start
  208.8 0.7 copy-start.7
  209.6 154.6 %all-gather.11.cloned.1.call-start = ((), (), s32[]{:S(2)}) async-start(), calls=%async_computation.3 | async-start | bytes 2359296 | tf_op jit(solution)/shard_map/all_gather | solution.py:307
  321.3 3.4 copy-start.1
  324.6 1.6 copy-start.3
  364.2 3.4 copy-start.2
  367.5 1.6 copy-start.4
Sparse Core Ops, SparseCore 0:
  208.2 55.6 all-gather.6
  266.4 54.7 all-gather.8
  323.1 41.0 all-gather.10

commit v2 on v1

v2 whole, which is shorter than its diff:
```python
import functools
import math

import jax
import jax.numpy as jnp
import numpy as np
from jax import lax
from jax.experimental import pallas as pl
from jax.experimental.pallas import tpu as pltpu
from jax.sharding import PartitionSpec as P

rope_base = 1000000.0
CHUNK_BLOCKS = 16
MIB = 1024 * 1024
PROJ_MIB = 24
ATT_MIB = 2
ATT_VMEM = 32
EARLY_PIECES = 5
VMEM = pl.BlockSpec(memory_space=pltpu.VMEM)
SMEM = pl.BlockSpec(memory_space=pltpu.SMEM)
ANY = pl.BlockSpec(memory_space=pl.ANY)


def angle_tables(positions, head_dim):
    half_dim = head_dim // 2
    inverse = rope_base ** (-2.0 * np.arange(half_dim) / head_dim)
    angles = positions[:, None] * inverse[None, :]
    cosine, sine = np.cos(angles), np.sin(angles)
    return (
        np.concatenate([cosine, cosine], axis=1).astype(np.float32),
        np.concatenate([-sine, sine], axis=1).astype(np.float32),
    )


def add_angles(cos_a, sin_a, cos_b, sin_b):
    return cos_a * cos_b - sin_a * sin_b, sin_a * cos_b + cos_a * sin_b


def rope(values, cosine, sine):
    return values * cosine + pltpu.roll(values, values.shape[-1] // 2, 1) * sine


def table_rows(block_rows, base_count):
    return (
        slice(0, block_rows),
        slice(block_rows, 2 * block_rows),
        2 * block_rows,
        2 * block_rows + base_count,
    )


def send_kernel(
    base_count,
    place_ref,
    seats_ref,
    lengths_ref,
    map_ref,
    table_ref,
    keys_ref,
    vals_ref,
    out_ref,
    held,
    tables,
    plan,
    plan_scalar,
    in_sems,
    out_sems,
    other_sems,
):
    count = held.shape[0]
    blocks_here, block_rows = keys_ref.shape[:2]
    block_count, sessions = map_ref.shape
    shift = blocks_here.bit_length() - 1
    lanes = plan.shape[1]
    get_tables = pltpu.make_async_copy(table_ref, tables, other_sems.at[0])
    get_tables.start()

    lengths = lengths_ref[...].astype(jnp.float32)
    block = lax.broadcasted_iota(jnp.int32, (block_count, sessions), 0)
    here = ((block * block_rows).astype(jnp.float32) < lengths) & (
        map_ref[...] >> shift == place_ref[0]
    )
    code = (block * blocks_here + (map_ref[...] & (blocks_here - 1))).astype(jnp.float32)
    lowest = jnp.min(jnp.where(here, code, 1e6), axis=0, keepdims=True)
    highest = jnp.max(jnp.where(here, code, -1.0), axis=0, keepdims=True)
    number = jnp.sum(jnp.where(here, 1.0, 0.0), axis=0, keepdims=True)

    seat_row = seats_ref[...].astype(jnp.float32)
    down = lax.broadcasted_iota(jnp.int32, (sessions, sessions), 0)
    along = lax.broadcasted_iota(jnp.int32, (sessions, sessions), 1)
    seat_column = jnp.sum(jnp.where(down == along, seat_row, 0.0), axis=1, keepdims=True)
    seated = seat_column == along.astype(jnp.float32)
    down = lax.broadcasted_iota(jnp.int32, (sessions, lanes), 0)
    along = lax.broadcasted_iota(jnp.int32, (sessions, lanes), 1)

    def by_seat(row):
        column = jnp.sum(jnp.where(seated, row, 0.0), axis=1, keepdims=True)
        return jnp.sum(jnp.where(down == along, column, 0.0), axis=0, keepdims=True)

    low, high, num = by_seat(lowest), by_seat(highest), by_seat(number)
    low_next, high_next, num_next = (pltpu.roll(x, lanes - 1, 1) for x in (low, high, num))
    first = jnp.where(num >= 1.0, low, jnp.where(num_next >= 1.0, low_next, -1.0))
    second = jnp.where(
        num >= 2.0,
        high,
        jnp.where(
            num >= 1.0,
            jnp.where(num_next >= 1.0, low_next, -1.0),
            jnp.where(num_next >= 2.0, high_next, -1.0),
        ),
    )
    even = lax.broadcasted_iota(jnp.int32, (1, lanes), 1) % 2 == 0
    plan[...] = jnp.where(even, first, pltpu.roll(second, 1, 1)).astype(jnp.int32)
    to_scalar = pltpu.make_async_copy(plan, plan_scalar, other_sems.at[1])
    to_scalar.start()
    to_scalar.wait()

    @pl.loop(0, count)
    def _(i):
        code = plan_scalar[0, i]

        @pl.when(code >= 0)
        def _():
            slot = code & (blocks_here - 1)
            pltpu.make_async_copy(keys_ref.at[slot], held.at[i, 0], in_sems.at[i]).start()
            pltpu.make_async_copy(vals_ref.at[slot], held.at[i, 1], in_sems.at[i]).start()

    get_tables.wait()
    row_cos, row_sin, base_cos, base_sin = table_rows(block_rows, base_count)

    @pl.loop(0, count)
    def _(i):
        code = plan_scalar[0, i]

        @pl.when(code >= 0)
        def _():
            pltpu.make_async_copy(held.at[i], held.at[i], in_sems.at[i]).wait()
            position = code >> shift
            cosine, sine = add_angles(
                tables[row_cos, :],
                tables[row_sin, :],
                tables[pl.ds(base_cos + position, 1), :],
                tables[pl.ds(base_sin + position, 1), :],
            )
            held[i, 0] = rope(held[i, 0].astype(jnp.float32), cosine, sine).astype(jnp.bfloat16)
            pltpu.make_async_copy(held.at[i], out_ref.at[i], out_sems.at[i]).start()

    @pl.loop(0, count)
    def _(i):
        @pl.when(plan_scalar[0, i] >= 0)
        def _():
            pltpu.make_async_copy(held.at[i], out_ref.at[i], out_sems.at[i]).wait()


def send_blocks(place, seats, lengths, map_t, table, base_count, pool_keys, pool_values, count):
    block_shape = pool_keys.shape[1:]
    return pl.pallas_call(
        functools.partial(send_kernel, base_count),
        out_shape=jax.ShapeDtypeStruct((count, 2) + block_shape, pool_keys.dtype),
        in_specs=[SMEM] + [VMEM] * 3 + [ANY] * 3,
        out_specs=ANY,
        scratch_shapes=[
            pltpu.VMEM((count, 2) + block_shape, pool_keys.dtype),
            pltpu.VMEM(table.shape, jnp.float32),
            pltpu.VMEM((1, 128), jnp.int32),
            pltpu.SMEM((1, 128), jnp.int32),
            pltpu.SemaphoreType.DMA((count,)),
            pltpu.SemaphoreType.DMA((count,)),
            pltpu.SemaphoreType.DMA((2,)),
        ],
        compiler_params=pltpu.CompilerParams(vmem_limit_bytes=60 * MIB),
        name="send_blocks",
    )(place, seats[None, :], lengths[None, :], map_t, table, pool_keys, pool_values)


def prepare_kernel(
    place_ref,
    seats_ref,
    lengths_ref,
    map_ref,
    tables,
    query_ref,
    key_ref,
    index_ref,
    own_ref,
    out_query_ref,
    out_key_ref,
    counts,
    *,
    base_count,
    blocks_here,
    capacity,
    block_rows,
):
    per_owner, heads, turn_len, head_dim = out_query_ref.shape
    block_count = index_ref.shape[1]
    shift = blocks_here.bit_length() - 1
    row_shift = block_rows.bit_length() - 1
    scaling = math.log2(math.e) / math.sqrt(head_dim)
    row_cos, row_sin, base_cos, base_sin = table_rows(block_rows, base_count)

    @pl.loop(0, counts.shape[0])
    def _(i):
        counts[i] = 0

    for seat in range(per_owner):
        session = seats_ref[place_ref[0] * per_owner + seat]
        length = lengths_ref[session]
        own_ref[seat] = length
        live = pl.cdiv(length, block_rows)

        @pl.loop(0, live)
        def _(j):
            source = map_ref[j, session] >> shift
            rank = counts[source]
            counts[source] = rank + 1
            index_ref[seat, j] = source * capacity + rank

        @pl.loop(live, block_count)
        def _(j):
            index_ref[seat, j] = index_ref[seat, 0]

        near = length & (block_rows - 1)
        far = length >> row_shift
        start_cos, start_sin = add_angles(
            tables[pl.ds(near, 1), :],
            tables[pl.ds(block_rows + near, 1), :],
            tables[pl.ds(base_cos + far, 1), :],
            tables[pl.ds(base_sin + far, 1), :],
        )
        for part in range(turn_len // block_rows):
            part_cos, part_sin = add_angles(
                start_cos,
                start_sin,
                tables[base_cos + part : base_cos + part + 1, :],
                tables[base_sin + part : base_sin + part + 1, :],
            )
            cosine, sine = add_angles(tables[row_cos, :], tables[row_sin, :], part_cos, part_sin)
            here = slice(part * block_rows, (part + 1) * block_rows)
            rows = slice(seat * turn_len + here.start, seat * turn_len + here.stop)
            key = key_ref[rows, :].astype(jnp.float32)
            out_key_ref[seat, here, :] = rope(key, cosine, sine).astype(jnp.bfloat16)
            cosine, sine = cosine * scaling, sine * scaling
            for h in range(heads):
                query = query_ref[rows, h * head_dim : (h + 1) * head_dim].astype(jnp.float32)
                out_query_ref[seat, h, here, :] = rope(query, cosine, sine).astype(jnp.bfloat16)


def prepare_turn(place, seats, lengths, map_t, table, base_count, turn_query, turn_key, sizes):
    pooled_count, blocks_here, capacity, per_owner, block_rows, head_dim = sizes
    turn_len = turn_query.shape[0] // per_owner
    heads = turn_query.shape[1] // head_dim
    block_count = map_t.shape[0]
    return pl.pallas_call(
        functools.partial(
            prepare_kernel,
            base_count=base_count,
            blocks_here=blocks_here,
            capacity=capacity,
            block_rows=block_rows,
        ),
        out_shape=(
            jax.ShapeDtypeStruct((per_owner, block_count), jnp.int32),
            jax.ShapeDtypeStruct((per_owner,), jnp.int32),
            jax.ShapeDtypeStruct((per_owner, heads, turn_len, head_dim), jnp.bfloat16),
            jax.ShapeDtypeStruct((per_owner, turn_len, head_dim), jnp.bfloat16),
        ),
        in_specs=[SMEM] * 4 + [VMEM] * 3,
        out_specs=(SMEM, SMEM, VMEM, VMEM),
        scratch_shapes=[pltpu.SMEM((pooled_count,), jnp.int32)],
        compiler_params=pltpu.CompilerParams(vmem_limit_bytes=16 * MIB),
        name="prepare_turn",
    )(place, seats, lengths, map_t, table, turn_query, turn_key)


def attention_kernel(
    seat,
    index_ref,
    length_ref,
    query_ref,
    turn_key_ref,
    turn_val_ref,
    arrived_ref,
    out_ref,
    blocks,
    top_ref,
    acc_ref,
    sems,
):
    _, heads, turn_len, head_dim = query_ref.shape
    _, _, block_rows, _ = blocks.shape
    chunk_rows = CHUNK_BLOCKS * block_rows
    length = length_ref[seat]
    chunks = pl.cdiv(length, chunk_rows)
    full = length // chunk_rows

    def copy(j):
        return pltpu.make_async_copy(arrived_ref.at[index_ref[seat, j]], blocks.at[j], sems.at[j])

    @pl.loop(0, chunks * CHUNK_BLOCKS, step=4)
    def _(j):
        for i in range(4):
            copy(j + i).start()

    def scores(h, keys):
        return lax.dot_general(
            query_ref[seat, h], keys, (((1,), (1,)), ((), ())), preferred_element_type=jnp.float32
        )

    def with_ones(vals):
        return jnp.concatenate([vals, jnp.ones(vals.shape, vals.dtype)], axis=1)

    rows = lax.broadcasted_iota(jnp.int32, (turn_len, turn_len), 0)
    cols = lax.broadcasted_iota(jnp.int32, (turn_len, turn_len), 1)
    new_keys = turn_key_ref[seat]
    new_vals = with_ones(turn_val_ref[seat * turn_len : (seat + 1) * turn_len, :])
    seen = [jnp.where(cols <= rows, scores(h, new_keys), -jnp.inf) for h in range(heads)]
    for h in range(heads):
        top = jnp.max(seen[h], axis=1, keepdims=True)
        weight = jnp.exp2(seen[h] - top).astype(jnp.bfloat16)
        top_ref[h] = top
        acc_ref[h] = jnp.dot(weight, new_vals, preferred_element_type=jnp.float32)

    def chunk_step(c, masked):
        first = c * CHUNK_BLOCKS

        @pl.loop(0, CHUNK_BLOCKS, step=4)
        def _(j):
            for i in range(4):
                copy(first + j + i).wait()

        keys = blocks[pl.ds(first, CHUNK_BLOCKS), 0].reshape(chunk_rows, head_dim)
        vals = with_ones(blocks[pl.ds(first, CHUNK_BLOCKS), 1].reshape(chunk_rows, head_dim))
        seen = [scores(h, keys) for h in range(heads)]
        if masked:
            place = c * chunk_rows + lax.broadcasted_iota(jnp.int32, seen[0].shape, 1)
            seen = [jnp.where(place < length, s, -jnp.inf) for s in seen]
        for h in range(heads):
            old = top_ref[h]
            top = jnp.maximum(old, jnp.max(seen[h], axis=1, keepdims=True))
            weight = jnp.exp2(seen[h] - top).astype(jnp.bfloat16)
            fade = jnp.exp2(old - top)
            top_ref[h] = top
            acc_ref[h] = acc_ref[h] * fade + jnp.dot(
                weight, vals, preferred_element_type=jnp.float32
            )

    @pl.loop(0, full)
    def _(c):
        chunk_step(c, False)

    @pl.when(full < chunks)
    def _():
        chunk_step(full, True)

    for h in range(heads):
        acc = acc_ref[h]
        out_ref[:, h * head_dim : (h + 1) * head_dim] = (
            acc[:, :head_dim] / acc[:, head_dim:]
        ).astype(jnp.bfloat16)


def attend(seat, recv_index, lengths, query, turn_key, turn_val, arrived):
    _, heads, turn_len, head_dim = query.shape
    block_rows = arrived.shape[2]
    block_count = recv_index.shape[1]
    keys_seen = block_count * block_rows + turn_len
    return pl.pallas_call(
        functools.partial(attention_kernel, seat),
        out_shape=jax.ShapeDtypeStruct((turn_len, heads * head_dim), jnp.bfloat16),
        in_specs=[SMEM] * 2 + [VMEM] * 3 + [ANY],
        out_specs=VMEM,
        scratch_shapes=[
            pltpu.VMEM((block_count, 2, block_rows, head_dim), jnp.bfloat16),
            pltpu.VMEM((heads, turn_len, 1), jnp.float32),
            pltpu.VMEM((heads, turn_len, 2 * head_dim), jnp.float32),
            pltpu.SemaphoreType.DMA((block_count,)),
        ],
        compiler_params=pltpu.CompilerParams(vmem_limit_bytes=ATT_VMEM * MIB),
        cost_estimate=pl.CostEstimate(
            flops=4 * heads * turn_len * keys_seen * head_dim,
            bytes_accessed=ATT_MIB * MIB,
            transcendentals=heads * turn_len * keys_seen,
        ),
        name="attend",
    )(recv_index, lengths, query, turn_key, turn_val, arrived)


def project_kernel(distances, started, place_ref, *refs):
    row_refs, refs = refs[:-5], refs[-5:]
    if started:
        row_refs, before_ref = row_refs[:-1], row_refs[-1]
    weight_ref, out_ref, held, rows, sems = refs
    pieces, _, width = held.shape
    depth = weight_ref.shape[1]
    count = len(distances)
    turn_len = row_refs[0].shape[0]
    tp = place_ref[0]
    groups = weight_ref.shape[0] // pieces

    def copy(i, j):
        home = weight_place(tp, (tp - distances[i]) & (groups - 1), j, pieces)
        return pltpu.make_async_copy(
            weight_ref.at[home], held.at[j, i * depth : (i + 1) * depth], sems.at[i, j]
        )

    for j in range(pieces):
        for i in range(count):
            copy(i, j).start()
    for k, row_ref in enumerate(row_refs):
        seat, i = divmod(k, count)
        rows[seat * turn_len : (seat + 1) * turn_len, i * depth : (i + 1) * depth] = row_ref[...]
    for j in range(pieces):
        for i in range(count):
            copy(i, j).wait()
        cols = slice(j * width, (j + 1) * width)
        for first in range(0, rows.shape[0], turn_len):
            here = slice(first, first + turn_len)
            part = jnp.dot(rows[here], held[j], preferred_element_type=jnp.float32)
            if started:
                part = part + before_ref[here, cols]
            out_ref[here, cols] = part.astype(out_ref.dtype)


def project(place, distances, gathered, before, weights, pieces, out_type):
    count = len(gathered[0])
    rows, depth = gathered[0][0].shape
    width = weights.shape[2]
    flat = [piece for seat in gathered for piece in seat]
    flat = flat if before is None else flat + [before]
    return pl.pallas_call(
        functools.partial(project_kernel, distances, before is not None),
        out_shape=jax.ShapeDtypeStruct((rows * len(gathered), pieces * width), out_type),
        in_specs=[SMEM] + [VMEM] * len(flat) + [pl.BlockSpec(memory_space=pltpu.HBM)],
        out_specs=VMEM,
        scratch_shapes=[
            pltpu.VMEM((pieces, count * depth, width), jnp.bfloat16),
            pltpu.VMEM((rows * len(gathered), count * depth), jnp.bfloat16),
            pltpu.SemaphoreType.DMA((count, pieces)),
        ],
        compiler_params=pltpu.CompilerParams(vmem_limit_bytes=PROJ_MIB * MIB),
        cost_estimate=pl.CostEstimate(
            flops=2 * rows * len(gathered) * count * depth * pieces * width,
            bytes_accessed=8 * MIB,
            transcendentals=0,
        ),
        name="project",
    )(place, *flat, weights)


def weight_place(plane, tp, rest, pieces):
    return (plane ^ tp) * pieces + rest


def spread_weights(out_weight, pieces):
    moves = []
    for p in range(lax.axis_size("pool")):
        for t in range(lax.axis_size("tp")):
            to = weight_place(p // pieces, t, p % pieces, pieces)
            moves.append((p * lax.axis_size("tp") + t, to * lax.axis_size("tp") + t))
    return lax.ppermute(out_weight, ("pool", "tp"), moves)


def to_planes(values, pieces):
    moves = []
    for p in range(lax.axis_size("pool")):
        for t in range(lax.axis_size("tp")):
            to = weight_place(p // pieces, t, p % pieces, pieces)
            moves.append((to * lax.axis_size("tp") + t, to * lax.axis_size("tp") + p // pieces))
    return lax.ppermute(values, ("pool", "tp"), moves)


def shift_tp(values, step):
    count = lax.axis_size("tp")
    return lax.ppermute(values, "tp", [(i, (i + step) % count) for i in range(count)])


def gather_ring(piece, farthest_from_left):
    count = lax.axis_size("tp")
    pieces, distances = [piece], [0]
    from_left = from_right = piece
    for distance in range(1, count // 2 + 1):
        last = 2 * distance == count
        if not last or farthest_from_left:
            from_left = shift_tp(from_left, 1)
            pieces.append(from_left)
            distances.append(distance)
        if not last or not farthest_from_left:
            from_right = shift_tp(from_right, -1)
            pieces.append(from_right)
            distances.append(-distance)
    return pieces, distances


def local(
    turn_query,
    turn_key,
    turn_value,
    pool_keys,
    pool_values,
    seat_session,
    history_len,
    block_map,
    out_weight,
):
    pooled_count = lax.axis_size("pool")
    tp_count = lax.axis_size("tp")
    place = lax.axis_index("pool")[None]
    blocks_here, rows_per_block, head_dim = pool_keys.shape
    block_count = block_map.shape[1]
    per_owner = seat_session.shape[0] // pooled_count
    capacity = per_owner * block_count // pooled_count
    pieces = pooled_count // tp_count

    base_count = block_count + 8
    table = jnp.asarray(
        np.concatenate(
            [
                *angle_tables(np.arange(rows_per_block), head_dim),
                *angle_tables(np.arange(base_count) * rows_per_block, head_dim),
            ]
        )
    )
    map_t = block_map.T

    spread = spread_weights(out_weight, pieces)
    sent = send_blocks(
        place,
        seat_session,
        history_len,
        map_t,
        table,
        base_count,
        pool_keys,
        pool_values,
        pooled_count * capacity,
    )
    sent, spread = lax.optimization_barrier((sent, spread))
    arrived = lax.all_to_all(sent, "pool", split_axis=0, concat_axis=0, tiled=True)

    turn_query, turn_key, _ = lax.optimization_barrier((turn_query, turn_key, sent))
    sizes = (pooled_count, blocks_here, capacity, per_owner, rows_per_block, head_dim)
    recv_index, own_lengths, queries, new_keys = prepare_turn(
        place, seat_session, history_len, map_t, table, base_count, turn_query, turn_key, sizes
    )
    moved = to_planes(spread, pieces)
    weights = lax.all_gather(moved, "pool", axis=0, tiled=False)

    gathered = []
    for seat in range(per_owner):
        attended = attend(seat, recv_index, own_lengths, queries, new_keys, turn_value, arrived)
        if gathered:
            attended, *_ = lax.optimization_barrier((attended, *gathered[-1][1:3]))
        ring, distances = gather_ring(attended, seat % 2 == 0)
        gathered.append(ring)
    early = EARLY_PIECES
    where = lax.axis_index("tp")[None]
    near, far = ([ring[:early] for ring in gathered], [ring[early:] for ring in gathered])
    partial = project(where, distances[:early], near, None, weights, pieces, jnp.float32)
    return project(where, distances[early:], far, partial, weights, pieces, jnp.bfloat16)


def solution(mesh):
    return jax.shard_map(
        local,
        mesh=mesh,
        in_specs=(
            P("pool", "tp"),
            P("pool", "tp"),
            P("pool", "tp"),
            P("pool", None, "tp"),
            P("pool", None, "tp"),
            P(),
            P(),
            P(),
            P("tp", "pool"),
        ),
        out_specs=P("pool", "tp"),
        check_vma=False,
    )
```

time: 388 us -> 173 us (0.45)
  Pallas kernels: 165 us -> 30.5 us
  waiting for transfers between devices: 178 us -> 67.4 us
  starting transfers between devices: 8.62 us -> 55.1 us
  local copies, waits for them, and re-layouts: 15.9 us -> 4.13 us
  other arithmetic: 6.1 us -> 0 us
    pallas_call x3 -> x4, Pallas kernels: 150 us -> 18.1 us  [the longest x2 8.93 us: project(): pl.pallas_call(functools.partial(project_kernel, distances, before is not...]
    all_gather x2 -> x0, waiting for transfers between devices: 74.8 us -> none  [local(): outputs.append(lax.all_gather(attended, 'tp', axis=0, tiled=False))]
    all_gather x1, waiting for transfers between devices: 57.4 us -> 0.01 us  [local(): weights = lax.all_gather(moved, 'pool', axis=0, tiled=False)]
    all_to_all x1, starting transfers between devices: 7.82 us -> 32.4 us  [local(): lax.all_to_all(sent, 'pool', split_axis=0, concat_axis=0, tiled=True)]
    ppermute x1 -> x16, starting transfers between devices: 0.68 us -> 22.7 us  [the longest x14 20.4 us: shift_tp(): lax.ppermute(values, 'tp', [(i, (i + step) % count) for i in range(count)])]
    ppermute x1 -> x16, waiting for transfers between devices: 0.01 us -> 15 us  [the longest x14 15 us: shift_tp(): lax.ppermute(values, 'tp', [(i, (i + step) % count) for i in range(count)])]
    unnamed x23 -> x20, local copies, waits for them, and re-layouts: 11.7 us -> 4.13 us
    all_to_all x1, waiting for transfers between devices: 46 us -> 52.4 us  [local(): lax.all_to_all(sent, 'pool', split_axis=0, concat_axis=0, tiled=True)]
  transfers between devices with their start and end apart: 5 -> 18, of which waited for: 4 -> 6; matrix products, arithmetic and copies ran while one was open for 2% -> 0% of each run, Pallas kernels for 4% -> 15%
where the time goes in v2:
time: 173 us; the launch traced here: 171 us
  waiting for transfers between devices  67.4 us (39%)
  starting transfers between devices  55.1 us (32%)
  Pallas kernels  30.5 us (18%)
  between operations  13.7 us (8%)
  local copies, waits for them, and re-layouts  4.13 us (2%)
    all_to_all x1, waiting for transfers between devices, local(): lax.all_to_all(sent, 'pool', split_axis=0, concat_axis=0, tiled=True)  52.4 us
    all_to_all x1, starting transfers between devices, local(): lax.all_to_all(sent, 'pool', split_axis=0, concat_axis=0, tiled=True)  32.4 us
    ppermute x14, starting transfers between devices, shift_tp(): lax.ppermute(values, 'tp', [(i, (i + step) % count) for i in range(count)])  20.4 us
    ppermute x14, waiting for transfers between devices, shift_tp(): lax.ppermute(values, 'tp', [(i, (i + step) % count) for i in range(count)])  15 us
    pallas_call x2, Pallas kernels, attend(): pl.pallas_call(functools.partial(attention_kernel, seat), out_shape=jax.S...  12.5 us
    pallas_call x2, Pallas kernels, project(): pl.pallas_call(functools.partial(project_kernel, distances, before is not...  8.93 us
    pallas_call x1, Pallas kernels, send_blocks(): pl.pallas_call(functools.partial(send_kernel, base_count), out_shape=jax....  6.64 us
    unnamed x20, local copies, waits for them, and re-layouts  4.13 us
  transfers between devices with their start and end apart: 18, of which 6 were waited for; matrix products, arithmetic and copies ran while one was open for 0% of the time, Pallas kernels for 15%

profile of v2, /device:TPU:2, one launch (start us, length us, event | category | flops | bytes accessed | tf_op | source)
XLA Modules:
  0.0 170.9 jit_solution(342184409569359477)
XLA Ops:
  6.5 0.0 all-gather.3.cloned.1.call-start
  6.5 1.6 collective-permute-start
  8.1 6.6 %send_blocks.1 = bf16[64,2,128,128]{3,2,1,0:T(8,128)(2,1)} custom-call(s32[1]{0:T(128)} %bitcast.1.place_ref, s32[1,64]{1,0:T(1,128)} %bitcast.10, s32[1,64]{1,0:T(1,128)} %bitcast.11, s32[32,64]{1,0:T(8,128)} %bitcast.8, f32[336,128]{1,0:T(8,128)} %constant.11.clone.table_ref.tables, bf16[64,128,128]{2,1,0:T(8,128)(2,1)} %keys_ref.1, ...), custom_call_target="tpu_custom_call" | custom-call | tf_op jit(solution)/shard_map/send_blocks/pallas_call | solution.py:157
  14.8 0.0 collective-permute-done
  14.8 0.7 collective-permute-start.15
  15.5 0.0 collective-permute-done.15
  15.5 0.0 copy-start.9
  15.5 0.7 copy-done.9
  16.2 0.0 all-gather.3.cloned.1.call-update
  16.2 0.0 copy-start.2
  16.2 0.0 copy-start.3
  16.2 0.0 copy-start.4
  16.3 0.0 copy-start.5
  16.3 0.0 copy-start.6
  16.3 0.0 copy-start.7
  16.3 0.0 copy-start.8
  16.3 32.4 %all-to-all-start = ((bf16[64,2,128,128]{3,2,1,0:T(8,128)(2,1)}), bf16[64,2,128,128]{3,2,1,0:T(8,128)(2,1)}, u32[]{:S(2)}, u32[]{:S(2)}) async-start(bf16[64,2,128,128]{3,2,1,0:T(8,128)(2,1)} %send_blocks.1), calls=%async_computation | async-start | bytes 8388608 | tf_op jit(solution)/shard_map/all_to_all | solution.py:539
  48.7 0.0 copy-done.2
  48.7 0.0 copy-done.3
  48.8 0.0 copy-done.4
  48.8 0.0 copy-done.5
  48.8 0.0 copy-done.6
  48.8 0.0 copy-done.7
  48.8 2.5 %prepare_turn.1 = (s32[2,32]{1,0:T(2,128)S(1)}, s32[2]{0:T(128)S(1)}, bf16[2,4,256,128]{3,2,1,0:T(8,128)(2,1)S(1)}, bf16[2,256,128]{2,1,0:T(8,128)(2,1)S(1)}) custom-call(s32[1]{0:T(128)} %bitcast.1.place_ref, s32[64]{0:T(128)S(1)} %copy-done.6, s32[64]{0:T(128)S(1)} %copy-done.7, s32[32,64]{1,0:T(8,128)S(1)} %bitcast.9, f32[336,128]{1,0:T(8,128)S(1)} %copy-done.2, ...), custom_call_target="tpu_custom_call" | custom-call | tf_op jit(solution)/shard_map/prepare_turn/pallas_call | solution.py:254
  51.3 52.4 %all-to-all-done.arrived_ref = bf16[64,2,128,128]{3,2,1,0:T(8,128)(2,1)} async-done(((bf16[64,2,128,128]{3,2,1,0:T(8,128)(2,1)}), bf16[64,2,128,128]{3,2,1,0:T(8,128)(2,1)}, u32[]{:S(2)}, u32[]{:S(2)}) %all-to-all-start) | async-done | bytes 4194336 | tf_op jit(solution)/shard_map/all_to_all | solution.py:539
  103.7 0.0 copy-done.8
  103.7 7.5 %attend.2.refs_0_ = bf16[256,512]{1,0:T(8,128)(2,1)S(1)} custom-call(s32[2,32]{1,0:T(2,128)S(1)} %get-tuple-element.17.index_ref, s32[2]{0:T(128)S(1)} %get-tuple-element.18.length_ref, bf16[2,4,256,128]{3,2,1,0:T(8,128)(2,1)S(1)} %get-tuple-element.19.query_ref, bf16[2,256,128]{2,1,0:T(8,128)(2,1)S(1)} %get-tuple-element.20.turn_key_ref, ...), custom_call_target="tpu_custom_call" | custom-call | flops 2281701376 | bytes 2097152 | tf_op jit(solution)/shard_map/attend/pallas_call | solution.py:368
  111.2 0.1 collective-permute-start.1
  111.3 3.2 %collective-permute-start.4 = (bf16[256,512]{1,0:T(8,128)(2,1)S(1)}, bf16[256,512]{1,0:T(8,128)(2,1)S(1)}, u32[]{:S(2)}, u32[]{:S(2)}) collective-permute-start(bf16[256,512]{1,0:T(8,128)(2,1)S(1)} %attend.2.refs_0_), channel_id=1, source_target_pairs={{0,7},{1,0},{2,1},{3,2},{4,3},{5,4},{6,5},{7,6},{8,15},{9,8},{10,9... | collective-permute-start | bytes 786440 | tf_op jit(solution)/shard_map/ppermute | solution.py:475
  114.6 5.0 %attend.3.refs_5_ = bf16[256,512]{1,0:T(8,128)(2,1)S(1)} custom-call(s32[2,32]{1,0:T(2,128)S(1)} %get-tuple-element.17.index_ref, s32[2]{0:T(128)S(1)} %get-tuple-element.18.length_ref, bf16[2,4,256,128]{3,2,1,0:T(8,128)(2,1)S(1)} %get-tuple-element.19.query_ref, bf16[2,256,128]{2,1,0:T(8,128)(2,1)S(1)} %get-tuple-element.20.turn_key_ref, ...), custom_call_target="tpu_custom_call" | custom-call | flops 2281701376 | bytes 2097152 | tf_op jit(solution)/shard_map/attend/pallas_call | solution.py:368
  119.5 0.0 collective-permute-done.1.refs_1_
  119.5 0.0 collective-permute-done.4.refs_2_
  119.6 2.6 %collective-permute-start.11 = (bf16[256,512]{1,0:T(8,128)(2,1)S(1)}, bf16[256,512]{1,0:T(8,128)(2,1)S(1)}, u32[]{:S(2)}, u32[]{:S(2)}) collective-permute-start(bf16[256,512]{1,0:T(8,128)(2,1)S(1)} %attend.3.refs_5_), channel_id=1, source_target_pairs={{0,7},{1,0},{2,1},{3,2},{4,3},{5,4},{6,5},{7,6},{8,15},{9,8},{10,9... | collective-permute-start | bytes 786440 | tf_op jit(solution)/shard_map/ppermute | solution.py:475
  122.2 0.0 collective-permute-start.8
  122.2 0.0 collective-permute-start.2
  122.2 4.9 %collective-permute-done.11.refs_7_ = bf16[256,512]{1,0:T(8,128)(2,1)S(1)} collective-permute-done((bf16[256,512]{1,0:T(8,128)(2,1)S(1)}, bf16[256,512]{1,0:T(8,128)(2,1)S(1)}, u32[]{:S(2)}, u32[]{:S(2)}) %collective-permute-start.11) | collective-permute-done | bytes 262176 | tf_op jit(solution)/shard_map/ppermute | solution.py:475
  127.1 3.5 %collective-permute-start.12 = (bf16[256,512]{1,0:T(8,128)(2,1)S(1)}, bf16[256,512]{1,0:T(8,128)(2,1)S(1)}, u32[]{:S(2)}, u32[]{:S(2)}) collective-permute-start(bf16[256,512]{1,0:T(8,128)(2,1)S(1)} %collective-permute-done.11.refs_7_), channel_id=1, source_target_pairs={{0,7},{1,0},{2,1},{3,2},{4,3},{5,4},{6,5},{7,6},{8,15},{9,8},{10,9... | collective-permute-start | bytes 786440 | tf_op jit(solution)/shard_map/ppermute | solution.py:475
  130.5 0.0 collective-permute-start.5
  130.5 1.0 collective-permute-done.8.refs_6_
  131.5 1.0 collective-permute-start.9
  132.5 4.6 %collective-permute-done.2.refs_3_ = bf16[256,512]{1,0:T(8,128)(2,1)S(1)} collective-permute-done((bf16[256,512]{1,0:T(8,128)(2,1)S(1)}, bf16[256,512]{1,0:T(8,128)(2,1)S(1)}, u32[]{:S(2)}, u32[]{:S(2)}) %collective-permute-start.2) | collective-permute-done | bytes 262176 | tf_op jit(solution)/shard_map/ppermute | solution.py:475
  137.1 0.0 collective-permute-start.3
  137.1 0.0 collective-permute-done.12.refs_9_
  137.1 3.2 %collective-permute-start.13 = (bf16[256,512]{1,0:T(8,128)(2,1)S(1)}, bf16[256,512]{1,0:T(8,128)(2,1)S(1)}, u32[]{:S(2)}, u32[]{:S(2)}) collective-permute-start(bf16[256,512]{1,0:T(8,128)(2,1)S(1)} %collective-permute-done.12.refs_9_), channel_id=1, source_target_pairs={{0,7},{1,0},{2,1},{3,2},{4,3},{5,4},{6,5},{7,6},{8,15},{9,8},{10,9... | collective-permute-start | bytes 786440 | tf_op jit(solution)/shard_map/ppermute | solution.py:475
  140.4 1.5 collective-permute-done.5.refs_4_
  141.9 3.5 %collective-permute-start.6 = (bf16[256,512]{1,0:T(8,128)(2,1)S(1)}, bf16[256,512]{1,0:T(8,128)(2,1)S(1)}, u32[]{:S(2)}, u32[]{:S(2)}) collective-permute-start(bf16[256,512]{1,0:T(8,128)(2,1)S(1)} %collective-permute-done.5.refs_4_), channel_id=1, source_target_pairs={{0,7},{1,0},{2,1},{3,2},{4,3},{5,4},{6,5},{7,6},{8,15},{9,8},{10,9... | collective-permute-start | bytes 786440 | tf_op jit(solution)/shard_map/ppermute | solution.py:475
  145.4 0.0 collective-permute-done.9.refs_8_
  145.4 0.0 collective-permute-start.10
  145.4 3.0 %collective-permute-done.3.refs_0_ = bf16[256,512]{1,0:T(8,128)(2,1)S(1)} collective-permute-done((bf16[256,512]{1,0:T(8,128)(2,1)S(1)}, bf16[256,512]{1,0:T(8,128)(2,1)S(1)}, u32[]{:S(2)}, u32[]{:S(2)}) %collective-permute-start.3) | collective-permute-done | bytes 262176 | tf_op jit(solution)/shard_map/ppermute | solution.py:475
  148.4 0.0 collective-permute-start.7
  148.4 0.0 collective-permute-done.13.refs_4_
  148.4 3.2 %collective-permute-start.14 = (bf16[256,512]{1,0:T(8,128)(2,1)S(1)}, bf16[256,512]{1,0:T(8,128)(2,1)}, u32[]{:S(2)}, u32[]{:S(2)}) collective-permute-start(bf16[256,512]{1,0:T(8,128)(2,1)S(1)} %collective-permute-done.13.refs_4_), channel_id=1, source_target_pairs={{0,7},{1,0},{2,1},{3,2},{4,3},{5,4},{6,5},{7,6},{8,15},{9,8},{10,9... | collective-permute-start | bytes 786440 | tf_op jit(solution)/shard_map/ppermute | solution.py:475
  151.6 0.0 all-gather.3.cloned.1.call-done
  151.6 0.0 copy-start
  151.6 3.4 %copy-done = bf16[16384,256]{1,0:T(8,128)(2,1)S(1)} copy-done((bf16[16384,256]{1,0:T(8,128)(2,1)S(1)}, bf16[16384,256]{1,0:T(8,128)(2,1)}, u32[]{:S(2)}) %copy-start) | copy-done | bytes 8388632
  155.0 0.0 copy-start.1
  155.0 4.1 %project.2.refs_6_ = f32[512,1024]{1,0:T(8,128)S(1)} custom-call(s32[1]{0:T(128)} %bitcast.place_ref, bf16[256,512]{1,0:T(8,128)(2,1)S(1)} %attend.2.refs_0_, bf16[256,512]{1,0:T(8,128)(2,1)S(1)} %collective-permute-done.1.refs_1_, bf16[256,512]{1,0:T(8,128)(2,1)S(1)} %collective-permute-done.4.refs_2_, bf16[256,512]{1,0:T(8,128)(2,1)S(1)} %collective-permute-done.2.refs_3_, ...), custom_call_target="tpu_custom_call" | custom-call | flops 2684354560 | bytes 8388608 | tf_op jit(solution)/shard_map/project/pallas_call | solution.py:431
  159.1 0.0 collective-permute-done.6.refs_1_
  159.1 0.0 collective-permute-done.10.refs_3_
  159.1 0.0 collective-permute-done.7.refs_2_
  159.1 0.0 collective-permute-done.14.refs_5_
  159.2 0.0 copy-done.1
  159.2 4.8 %project.3 = bf16[512,1024]{1,0:T(8,128)(2,1)} custom-call(s32[1]{0:T(128)} %bitcast.place_ref, bf16[256,512]{1,0:T(8,128)(2,1)S(1)} %collective-permute-done.3.refs_0_, bf16[256,512]{1,0:T(8,128)(2,1)S(1)} %collective-permute-done.6.refs_1_, bf16[256,512]{1,0:T(8,128)(2,1)} %collective-permute-done.7.refs_2_, ...), custom_call_target="tpu_custom_call" | custom-call | flops 1610612736 | bytes 8388608 | tf_op jit(solution)/shard_map/project/pallas_call | solution.py:431
Async XLA Ops:
  6.5 145.1 %all-gather.3.cloned.1.call-start = ((), (), s32[]{:S(2)}) async-start(), calls=%async_computation.1 | async-start | bytes 8650752 | tf_op jit(solution)/shard_map/all_gather | solution.py:547
  6.5 8.2 %collective-permute-start = (bf16[512,256]{1,0:T(8,128)(2,1)}, bf16[512,256]{1,0:T(8,128)(2,1)S(1)}, u32[]{:S(2)}, u32[]{:S(2)}) collective-permute-start(bf16[512,256]{1,0:T(8,128)(2,1)} %param.18), channel_id=1, source_target_pairs={{0,0},{1,33},{2,66},{3,99},{4,132},{5,165},{6,198},{7,231},{8,8},{... | collective-permute-start | bytes 786440 | tf_op jit(solution)/shard_map/ppermute | solution.py:461
  14.8 0.7 collective-permute-start.15
  15.5 0.7 copy-start.9
  16.2 32.5 %copy-start.2 = (f32[336,128]{1,0:T(8,128)S(1)}, f32[336,128]{1,0:T(8,128)}, u32[]{:S(2)}) copy-start(f32[336,128]{1,0:T(8,128)} %constant.11.clone.table_ref.tables) | copy-start | bytes 516100
  16.2 32.5 %copy-start.3 = (bf16[512,512]{1,0:T(8,128)(2,1)S(1)}, bf16[512,512]{1,0:T(8,128)(2,1)}, u32[]{:S(2)}) copy-start(bf16[512,512]{1,0:T(8,128)(2,1)} %query_ref) | copy-start | bytes 1572868
  16.2 32.5 %copy-start.4 = (bf16[512,128]{1,0:T(8,128)(2,1)S(1)}, bf16[512,128]{1,0:T(8,128)(2,1)}, u32[]{:S(2)}) copy-start(bf16[512,128]{1,0:T(8,128)(2,1)} %key_ref) | copy-start | bytes 393220
  16.3 32.5 %copy-start.5 = (s32[64,32]{0,1:T(8,128)S(1)}, s32[64,32]{0,1:T(8,128)}, u32[]{:S(2)}) copy-start(s32[64,32]{0,1:T(8,128)} %param.17) | copy-start | bytes 24580
  16.3 32.5 %copy-start.6 = (s32[64]{0:T(128)S(1)}, s32[64]{0:T(128)}, u32[]{:S(2)}) copy-start(s32[64]{0:T(128)} %seats_ref.1) | copy-start | bytes 772
  16.3 32.5 %copy-start.7 = (s32[64]{0:T(128)S(1)}, s32[64]{0:T(128)}, u32[]{:S(2)}) copy-start(s32[64]{0:T(128)} %lengths_ref.1) | copy-start | bytes 772
  16.3 87.4 %copy-start.8 = (bf16[512,128]{1,0:T(8,128)(2,1)S(1)}, bf16[512,128]{1,0:T(8,128)(2,1)}, u32[]{:S(2)}) copy-start(bf16[512,128]{1,0:T(8,128)(2,1)} %turn_val_ref.3) | copy-start | bytes 393220
  16.3 87.4 %all-to-all-start = ((bf16[64,2,128,128]{3,2,1,0:T(8,128)(2,1)}), bf16[64,2,128,128]{3,2,1,0:T(8,128)(2,1)}, u32[]{:S(2)}, u32[]{:S(2)}) async-start(bf16[64,2,128,128]{3,2,1,0:T(8,128)(2,1)} %send_blocks.1), calls=%async_computation | async-start | bytes 8388608 | tf_op jit(solution)/shard_map/all_to_all | solution.py:539
  111.2 8.3 %collective-permute-start.1 = (bf16[256,512]{1,0:T(8,128)(2,1)S(1)}, bf16[256,512]{1,0:T(8,128)(2,1)S(1)}, u32[]{:S(2)}, u32[]{:S(2)}) collective-permute-start(bf16[256,512]{1,0:T(8,128)(2,1)S(1)} %attend.2.refs_0_), channel_id=1, source_target_pairs={{0,1},{1,2},{2,3},{3,4},{4,5},{5,6},{6,7},{7,0},{8,9},{9,10},{10,1... | collective-permute-start | bytes 786440 | tf_op jit(solution)/shard_map/ppermute | solution.py:475
  111.3 8.2 %collective-permute-start.4 = (bf16[256,512]{1,0:T(8,128)(2,1)S(1)}, bf16[256,512]{1,0:T(8,128)(2,1)S(1)}, u32[]{:S(2)}, u32[]{:S(2)}) collective-permute-start(bf16[256,512]{1,0:T(8,128)(2,1)S(1)} %attend.2.refs_0_), channel_id=1, source_target_pairs={{0,7},{1,0},{2,1},{3,2},{4,3},{5,4},{6,5},{7,6},{8,15},{9,8},{10,9... | collective-permute-start | bytes 786440 | tf_op jit(solution)/shard_map/ppermute | solution.py:475
  119.6 7.5 %collective-permute-start.11 = (bf16[256,512]{1,0:T(8,128)(2,1)S(1)}, bf16[256,512]{1,0:T(8,128)(2,1)S(1)}, u32[]{:S(2)}, u32[]{:S(2)}) collective-permute-start(bf16[256,512]{1,0:T(8,128)(2,1)S(1)} %attend.3.refs_5_), channel_id=1, source_target_pairs={{0,7},{1,0},{2,1},{3,2},{4,3},{5,4},{6,5},{7,6},{8,15},{9,8},{10,9... | collective-permute-start | bytes 786440 | tf_op jit(solution)/shard_map/ppermute | solution.py:475
  122.2 9.3 %collective-permute-start.8 = (bf16[256,512]{1,0:T(8,128)(2,1)S(1)}, bf16[256,512]{1,0:T(8,128)(2,1)S(1)}, u32[]{:S(2)}, u32[]{:S(2)}) collective-permute-start(bf16[256,512]{1,0:T(8,128)(2,1)S(1)} %attend.3.refs_5_), channel_id=1, source_target_pairs={{0,1},{1,2},{2,3},{3,4},{4,5},{5,6},{6,7},{7,0},{8,9},{9,10},{10,1... | collective-permute-start | bytes 786440 | tf_op jit(solution)/shard_map/ppermute | solution.py:475
  122.2 14.9 %collective-permute-start.2 = (bf16[256,512]{1,0:T(8,128)(2,1)S(1)}, bf16[256,512]{1,0:T(8,128)(2,1)S(1)}, u32[]{:S(2)}, u32[]{:S(2)}) collective-permute-start(bf16[256,512]{1,0:T(8,128)(2,1)S(1)} %collective-permute-done.1.refs_1_), channel_id=1, source_target_pairs={{0,1},{1,2},{2,3},{3,4},{4,5},{5,6},{6,7},{7,0},{8,9},{9,10},{10,1... | collective-permute-start | bytes 786440 | tf_op jit(solution)/shard_map/ppermute | solution.py:475
  127.1 10.1 %collective-permute-start.12 = (bf16[256,512]{1,0:T(8,128)(2,1)S(1)}, bf16[256,512]{1,0:T(8,128)(2,1)S(1)}, u32[]{:S(2)}, u32[]{:S(2)}) collective-permute-start(bf16[256,512]{1,0:T(8,128)(2,1)S(1)} %collective-permute-done.11.refs_7_), channel_id=1, source_target_pairs={{0,7},{1,0},{2,1},{3,2},{4,3},{5,4},{6,5},{7,6},{8,15},{9,8},{10,9... | collective-permute-start | bytes 786440 | tf_op jit(solution)/shard_map/ppermute | solution.py:475
  130.5 11.4 %collective-permute-start.5 = (bf16[256,512]{1,0:T(8,128)(2,1)S(1)}, bf16[256,512]{1,0:T(8,128)(2,1)S(1)}, u32[]{:S(2)}, u32[]{:S(2)}) collective-permute-start(bf16[256,512]{1,0:T(8,128)(2,1)S(1)} %collective-permute-done.4.refs_2_), channel_id=1, source_target_pairs={{0,7},{1,0},{2,1},{3,2},{4,3},{5,4},{6,5},{7,6},{8,15},{9,8},{10,9... | collective-permute-start | bytes 786440 | tf_op jit(solution)/shard_map/ppermute | solution.py:475
  131.5 13.9 %collective-permute-start.9 = (bf16[256,512]{1,0:T(8,128)(2,1)S(1)}, bf16[256,512]{1,0:T(8,128)(2,1)S(1)}, u32[]{:S(2)}, u32[]{:S(2)}) collective-permute-start(bf16[256,512]{1,0:T(8,128)(2,1)S(1)} %collective-permute-done.8.refs_6_), channel_id=1, source_target_pairs={{0,1},{1,2},{2,3},{3,4},{4,5},{5,6},{6,7},{7,0},{8,9},{9,10},{10,1... | collective-permute-start | bytes 786440 | tf_op jit(solution)/shard_map/ppermute | solution.py:475
  137.1 11.2 %collective-permute-start.3 = (bf16[256,512]{1,0:T(8,128)(2,1)S(1)}, bf16[256,512]{1,0:T(8,128)(2,1)S(1)}, u32[]{:S(2)}, u32[]{:S(2)}) collective-permute-start(bf16[256,512]{1,0:T(8,128)(2,1)S(1)} %collective-permute-done.2.refs_3_), channel_id=1, source_target_pairs={{0,1},{1,2},{2,3},{3,4},{4,5},{5,6},{6,7},{7,0},{8,9},{9,10},{10,1... | collective-permute-start | bytes 786440 | tf_op jit(solution)/shard_map/ppermute | solution.py:475
  137.1 11.2 %collective-permute-start.13 = (bf16[256,512]{1,0:T(8,128)(2,1)S(1)}, bf16[256,512]{1,0:T(8,128)(2,1)S(1)}, u32[]{:S(2)}, u32[]{:S(2)}) collective-permute-start(bf16[256,512]{1,0:T(8,128)(2,1)S(1)} %collective-permute-done.12.refs_9_), channel_id=1, source_target_pairs={{0,7},{1,0},{2,1},{3,2},{4,3},{5,4},{6,5},{7,6},{8,15},{9,8},{10,9... | collective-permute-start | bytes 786440 | tf_op jit(solution)/shard_map/ppermute | solution.py:475
  141.9 17.2 %collective-permute-start.6 = (bf16[256,512]{1,0:T(8,128)(2,1)S(1)}, bf16[256,512]{1,0:T(8,128)(2,1)S(1)}, u32[]{:S(2)}, u32[]{:S(2)}) collective-permute-start(bf16[256,512]{1,0:T(8,128)(2,1)S(1)} %collective-permute-done.5.refs_4_), channel_id=1, source_target_pairs={{0,7},{1,0},{2,1},{3,2},{4,3},{5,4},{6,5},{7,6},{8,15},{9,8},{10,9... | collective-permute-start | bytes 786440 | tf_op jit(solution)/shard_map/ppermute | solution.py:475
  145.4 13.8 %collective-permute-start.10 = (bf16[256,512]{1,0:T(8,128)(2,1)S(1)}, bf16[256,512]{1,0:T(8,128)(2,1)}, u32[]{:S(2)}, u32[]{:S(2)}) collective-permute-start(bf16[256,512]{1,0:T(8,128)(2,1)S(1)} %collective-permute-done.9.refs_8_), channel_id=1, source_target_pairs={{0,1},{1,2},{2,3},{3,4},{4,5},{5,6},{6,7},{7,0},{8,9},{9,10},{10,1... | collective-permute-start | bytes 786440 | tf_op jit(solution)/shard_map/ppermute | solution.py:475
  148.4 10.8 %collective-permute-start.7 = (bf16[256,512]{1,0:T(8,128)(2,1)S(1)}, bf16[256,512]{1,0:T(8,128)(2,1)}, u32[]{:S(2)}, u32[]{:S(2)}) collective-permute-start(bf16[256,512]{1,0:T(8,128)(2,1)S(1)} %collective-permute-done.3.refs_0_), channel_id=1, source_target_pairs={{0,1},{1,2},{2,3},{3,4},{4,5},{5,6},{6,7},{7,0},{8,9},{9,10},{10,1... | collective-permute-start | bytes 786440 | tf_op jit(solution)/shard_map/ppermute | solution.py:475
  148.4 10.8 %collective-permute-start.14 = (bf16[256,512]{1,0:T(8,128)(2,1)S(1)}, bf16[256,512]{1,0:T(8,128)(2,1)}, u32[]{:S(2)}, u32[]{:S(2)}) collective-permute-start(bf16[256,512]{1,0:T(8,128)(2,1)S(1)} %collective-permute-done.13.refs_4_), channel_id=1, source_target_pairs={{0,7},{1,0},{2,1},{3,2},{4,3},{5,4},{6,5},{7,6},{8,15},{9,8},{10,9... | collective-permute-start | bytes 786440 | tf_op jit(solution)/shard_map/ppermute | solution.py:475
  151.6 3.4 %copy-start = (bf16[16384,256]{1,0:T(8,128)(2,1)S(1)}, bf16[16384,256]{1,0:T(8,128)(2,1)}, u32[]{:S(2)}) copy-start(bf16[16384,256]{1,0:T(8,128)(2,1)} %all-gather.3.cloned.1.call-done) | copy-start | bytes 25165828
  155.0 4.2 %copy-start.1 = (bf16[16384,256]{1,0:T(8,128)(2,1)S(1)}, bf16[16384,256]{1,0:T(8,128)(2,1)}, u32[]{:S(2)}) copy-start(bf16[16384,256]{1,0:T(8,128)(2,1)} %all-gather.3.cloned.1.call-done) | copy-start | bytes 25165828
Sparse Core Ops, SparseCore 0:
  16.3 116.4 all-gather.2

commit v3 on v2

--- a/solution.py
+++ b/solution.py
@@ -12,10 +12,10 @@
 rope_base = 1000000.0
 CHUNK_BLOCKS = 16
 MIB = 1024 * 1024
-PROJ_MIB = 24
+PROJ_MIB = 52
 ATT_MIB = 2
 ATT_VMEM = 32
-EARLY_PIECES = 5
+EARLY_PIECES = 0
 VMEM = pl.BlockSpec(memory_space=pltpu.VMEM)
 SMEM = pl.BlockSpec(memory_space=pltpu.SMEM)
 ANY = pl.BlockSpec(memory_space=pl.ANY)
@@ -544,6 +544,7 @@
         place, seat_session, history_len, map_t, table, base_count, turn_query, turn_key, sizes
     )
     moved = to_planes(spread, pieces)
+    moved, arrived, queries = lax.optimization_barrier((moved, arrived, queries))
     weights = lax.all_gather(moved, "pool", axis=0, tiled=False)
 
     gathered = []
@@ -555,6 +556,8 @@
         gathered.append(ring)
     early = EARLY_PIECES
     where = lax.axis_index("tp")[None]
+    if early == 0:
+        return project(where, distances, gathered, None, weights, pieces, jnp.bfloat16)
     near, far = ([ring[:early] for ring in gathered], [ring[early:] for ring in gathered])
     partial = project(where, distances[:early], near, None, weights, pieces, jnp.float32)
     return project(where, distances[early:], far, partial, weights, pieces, jnp.bfloat16)

time: 173 us -> 157 us (0.908)
  starting transfers between devices: 55.1 us -> 41.4 us
  local copies, waits for them, and re-layouts: 4.13 us -> 0.07 us
  waiting for transfers between devices: 67.4 us -> 71.3 us
    all_to_all x1, starting transfers between devices: 32.4 us -> 8.16 us  [local(): lax.all_to_all(sent, 'pool', split_axis=0, concat_axis=0, tiled=True)]
    ppermute x14, starting transfers between devices: 20.4 us -> 30.9 us  [shift_tp(): lax.ppermute(values, 'tp', [(i, (i + step) % count) for i in range(count)])]
    ppermute x14, waiting for transfers between devices: 15 us -> 23.1 us  [shift_tp(): lax.ppermute(values, 'tp', [(i, (i + step) % count) for i in range(count)])]
    all_to_all x1, waiting for transfers between devices: 52.4 us -> 48.2 us  [local(): lax.all_to_all(sent, 'pool', split_axis=0, concat_axis=0, tiled=True)]
    unnamed x20 -> x28, local copies, waits for them, and re-layouts: 4.13 us -> 0.07 us
    pallas_call x2, Pallas kernels: 12.5 us -> 10.2 us  [attend(): pl.pallas_call(functools.partial(attention_kernel, seat), out_shape=jax.S...]
    pallas_call x2 -> x1, Pallas kernels: 8.93 us -> 9.41 us  [project(): pl.pallas_call(functools.partial(project_kernel, distances, before is not...]
  transfers between devices with their start and end apart: 18 -> 18, of which waited for: 6 -> 12; matrix products, arithmetic and copies ran while one was open for 0% -> 0% of each run, Pallas kernels for 15% -> 12%
where the time goes in v3:
time: 157 us; the launch traced here: 155 us
  waiting for transfers between devices  71.3 us (45%)
  starting transfers between devices  41.4 us (26%)
  Pallas kernels  28.8 us (18%)
  between operations  13.7 us (9%)
    all_to_all x1, waiting for transfers between devices, local(): lax.all_to_all(sent, 'pool', split_axis=0, concat_axis=0, tiled=True)  48.2 us
    ppermute x14, starting transfers between devices, shift_tp(): lax.ppermute(values, 'tp', [(i, (i + step) % count) for i in range(count)])  30.9 us
    ppermute x14, waiting for transfers between devices, shift_tp(): lax.ppermute(values, 'tp', [(i, (i + step) % count) for i in range(count)])  23.1 us
    pallas_call x2, Pallas kernels, attend(): pl.pallas_call(functools.partial(attention_kernel, seat), out_shape=jax.S...  10.2 us
    pallas_call x1, Pallas kernels, project(): pl.pallas_call(functools.partial(project_kernel, distances, before is not...  9.41 us
    all_to_all x1, starting transfers between devices, local(): lax.all_to_all(sent, 'pool', split_axis=0, concat_axis=0, tiled=True)  8.16 us
    pallas_call x1, Pallas kernels, send_blocks(): pl.pallas_call(functools.partial(send_kernel, base_count), out_shape=jax....  6.79 us
  transfers between devices with their start and end apart: 18, of which 12 were waited for; matrix products, arithmetic and copies ran while one was open for 0% of the time, Pallas kernels for 12%

profile of v3, /device:TPU:2, one launch (start us, length us, event | category | flops | bytes accessed | tf_op | source)
XLA Modules:
  0.0 155.2 jit_solution(8556976856382815369)
XLA Ops:
  6.5 1.6 %collective-permute-start = (bf16[512,256]{1,0:T(8,128)(2,1)}, bf16[512,256]{1,0:T(8,128)(2,1)S(1)}, u32[]{:S(2)}, u32[]{:S(2)}) collective-permute-start(bf16[512,256]{1,0:T(8,128)(2,1)} %param.18), channel_id=1, source_target_pairs={{0,0},{1,33},{2,66},{3,99},{4,132},{5,165},{6,198},{7,231},{8,8},{... | collective-permute-start | bytes 786440 | tf_op jit(solution)/shard_map/ppermute | solution.py:461
  8.1 6.8 %send_blocks.1 = bf16[64,2,128,128]{3,2,1,0:T(8,128)(2,1)} custom-call(s32[1]{0:T(128)} %bitcast.1.place_ref, s32[1,64]{1,0:T(1,128)} %bitcast.8, s32[1,64]{1,0:T(1,128)} %bitcast.9, s32[32,64]{1,0:T(8,128)} %bitcast.6, f32[336,128]{1,0:T(8,128)} %constant.11.clone.table_ref.tables, bf16[64,128,128]{2,1,0:T(8,128)(2,1)} %keys_ref.1, ...), custom_call_target="tpu_custom_call" | custom-call | tf_op jit(solution)/shard_map/send_blocks/pallas_call | solution.py:157
  14.9 0.0 copy-start
  14.9 0.0 copy-start.1
  14.9 0.0 copy-start.2
  15.0 0.0 copy-start.3
  15.0 0.0 copy-start.4
  15.0 0.0 copy-start.5
  15.0 0.0 copy-start.7
  15.0 0.0 collective-permute-done
  15.0 8.2 %all-to-all-start = ((bf16[64,2,128,128]{3,2,1,0:T(8,128)(2,1)}), bf16[64,2,128,128]{3,2,1,0:T(8,128)(2,1)}, u32[]{:S(2)}, u32[]{:S(2)}) async-start(bf16[64,2,128,128]{3,2,1,0:T(8,128)(2,1)} %send_blocks.1), calls=%async_computation | async-start | bytes 8388608 | tf_op jit(solution)/shard_map/all_to_all | solution.py:539
  23.2 0.0 all-gather.3.cloned.1.call-start
  23.2 0.7 collective-permute-start.1
  23.9 0.0 copy-done
  23.9 0.0 copy-done.1
  23.9 0.0 copy-done.2
  24.0 0.0 copy-done.3
  24.0 0.0 copy-done.4
  24.0 0.0 copy-done.5
  24.0 2.4 %prepare_turn.1 = (s32[2,32]{1,0:T(2,128)S(1)}, s32[2]{0:T(128)S(1)}, bf16[2,4,256,128]{3,2,1,0:T(8,128)(2,1)S(1)}, bf16[2,256,128]{2,1,0:T(8,128)(2,1)S(1)}) custom-call(s32[1]{0:T(128)} %bitcast.1.place_ref, s32[64]{0:T(128)S(1)} %copy-done.4, s32[64]{0:T(128)S(1)} %copy-done.5, s32[32,64]{1,0:T(8,128)S(1)} %bitcast.7, f32[336,128]{1,0:T(8,128)S(1)} %copy-done, ...), custom_call_target="tpu_custom_call" | custom-call | tf_op jit(solution)/shard_map/prepare_turn/pallas_call | solution.py:254
  26.4 0.0 collective-permute-done.1
  26.4 0.0 copy-start.8
  26.4 48.2 %all-to-all-done.arrived_ref = bf16[64,2,128,128]{3,2,1,0:T(8,128)(2,1)} async-done(((bf16[64,2,128,128]{3,2,1,0:T(8,128)(2,1)}), bf16[64,2,128,128]{3,2,1,0:T(8,128)(2,1)}, u32[]{:S(2)}, u32[]{:S(2)}) %all-to-all-start) | async-done | bytes 4194336 | tf_op jit(solution)/shard_map/all_to_all | solution.py:539
  74.6 0.0 copy-done.8
  74.6 0.0 all-gather.3.cloned.1.call-update
  74.6 0.0 copy-done.7
  74.6 4.9 %attend.2.refs_0_ = bf16[256,512]{1,0:T(8,128)(2,1)S(1)} custom-call(s32[2,32]{1,0:T(2,128)S(1)} %get-tuple-element.20.index_ref, s32[2]{0:T(128)S(1)} %get-tuple-element.21.length_ref, bf16[2,4,256,128]{3,2,1,0:T(8,128)(2,1)S(1)} %get-tuple-element.24.query_ref, bf16[2,256,128]{2,1,0:T(8,128)(2,1)S(1)} %get-tuple-element.25.turn_key_ref, ...), custom_call_target="tpu_custom_call" | custom-call | flops 2281701376 | bytes 2097152 | tf_op jit(solution)/shard_map/attend/pallas_call | solution.py:368
  79.5 4.7 %collective-permute-start.2 = (bf16[256,512]{1,0:T(8,128)(2,1)S(1)}, bf16[256,512]{1,0:T(8,128)(2,1)S(1)}, u32[]{:S(2)}, u32[]{:S(2)}) collective-permute-start(bf16[256,512]{1,0:T(8,128)(2,1)S(1)} %attend.2.refs_0_), channel_id=1, source_target_pairs={{0,1},{1,2},{2,3},{3,4},{4,5},{5,6},{6,7},{7,0},{8,9},{9,10},{10,1... | collective-permute-start | bytes 786440 | tf_op jit(solution)/shard_map/ppermute | solution.py:475
  84.2 6.0 %collective-permute-start.3 = (bf16[256,512]{1,0:T(8,128)(2,1)S(1)}, bf16[256,512]{1,0:T(8,128)(2,1)S(1)}, u32[]{:S(2)}, u32[]{:S(2)}) collective-permute-start(bf16[256,512]{1,0:T(8,128)(2,1)S(1)} %attend.2.refs_0_), channel_id=1, source_target_pairs={{0,7},{1,0},{2,1},{3,2},{4,3},{5,4},{6,5},{7,6},{8,15},{9,8},{10,9... | collective-permute-start | bytes 786440 | tf_op jit(solution)/shard_map/ppermute | solution.py:475
  90.1 5.3 %attend.3.refs_8_ = bf16[256,512]{1,0:T(8,128)(2,1)S(1)} custom-call(s32[2,32]{1,0:T(2,128)S(1)} %get-tuple-element.20.index_ref, s32[2]{0:T(128)S(1)} %get-tuple-element.21.length_ref, bf16[2,4,256,128]{3,2,1,0:T(8,128)(2,1)S(1)} %get-tuple-element.24.query_ref, bf16[2,256,128]{2,1,0:T(8,128)(2,1)S(1)} %get-tuple-element.25.turn_key_ref, ...), custom_call_target="tpu_custom_call" | custom-call | flops 2281701376 | bytes 2097152 | tf_op jit(solution)/shard_map/attend/pallas_call | solution.py:368
  95.4 0.0 copy-start.6
  95.4 0.2 collective-permute-done.2.refs_1_
  95.6 0.0 collective-permute-done.3.refs_2_
  95.7 3.6 %collective-permute-start.10 = (bf16[256,512]{1,0:T(8,128)(2,1)S(1)}, bf16[256,512]{1,0:T(8,128)(2,1)S(1)}, u32[]{:S(2)}, u32[]{:S(2)}) collective-permute-start(bf16[256,512]{1,0:T(8,128)(2,1)S(1)} %attend.3.refs_8_), channel_id=1, source_target_pairs={{0,7},{1,0},{2,1},{3,2},{4,3},{5,4},{6,5},{7,6},{8,15},{9,8},{10,9... | collective-permute-start | bytes 786440 | tf_op jit(solution)/shard_map/ppermute | solution.py:475
  99.3 0.0 collective-permute-start.9
  99.3 0.0 collective-permute-start.4
  99.3 6.3 %collective-permute-done.10.refs_10_ = bf16[256,512]{1,0:T(8,128)(2,1)S(1)} collective-permute-done((bf16[256,512]{1,0:T(8,128)(2,1)S(1)}, bf16[256,512]{1,0:T(8,128)(2,1)S(1)}, u32[]{:S(2)}, u32[]{:S(2)}) %collective-permute-start.10) | collective-permute-done | bytes 262176 | tf_op jit(solution)/shard_map/ppermute | solution.py:475
  105.6 3.7 %collective-permute-start.12 = (bf16[256,512]{1,0:T(8,128)(2,1)S(1)}, bf16[256,512]{1,0:T(8,128)(2,1)S(1)}, u32[]{:S(2)}, u32[]{:S(2)}) collective-permute-start(bf16[256,512]{1,0:T(8,128)(2,1)S(1)} %collective-permute-done.10.refs_10_), channel_id=1, source_target_pairs={{0,7},{1,0},{2,1},{3,2},{4,3},{5,4},{6,5},{7,6},{8,15},{9,8},{10,9... | collective-permute-start | bytes 786440 | tf_op jit(solution)/shard_map/ppermute | solution.py:475
  109.3 0.1 collective-permute-start.5
  109.3 0.1 collective-permute-done.9.refs_9_
  109.5 1.8 %collective-permute-start.11 = (bf16[256,512]{1,0:T(8,128)(2,1)S(1)}, bf16[256,512]{1,0:T(8,128)(2,1)S(1)}, u32[]{:S(2)}, u32[]{:S(2)}) collective-permute-start(bf16[256,512]{1,0:T(8,128)(2,1)S(1)} %collective-permute-done.9.refs_9_), channel_id=1, source_target_pairs={{0,1},{1,2},{2,3},{3,4},{4,5},{5,6},{6,7},{7,0},{8,9},{9,10},{10,1... | collective-permute-start | bytes 786440 | tf_op jit(solution)/shard_map/ppermute | solution.py:475
  111.3 3.8 %collective-permute-done.4.refs_3_ = bf16[256,512]{1,0:T(8,128)(2,1)S(1)} collective-permute-done((bf16[256,512]{1,0:T(8,128)(2,1)S(1)}, bf16[256,512]{1,0:T(8,128)(2,1)S(1)}, u32[]{:S(2)}, u32[]{:S(2)}) %collective-permute-start.4) | collective-permute-done | bytes 262176 | tf_op jit(solution)/shard_map/ppermute | solution.py:475
  115.1 0.0 collective-permute-start.6
  115.1 0.8 collective-permute-done.12.refs_12_
  115.9 3.7 %collective-permute-start.14 = (bf16[256,512]{1,0:T(8,128)(2,1)S(1)}, bf16[256,512]{1,0:T(8,128)(2,1)S(1)}, u32[]{:S(2)}, u32[]{:S(2)}) collective-permute-start(bf16[256,512]{1,0:T(8,128)(2,1)S(1)} %collective-permute-done.12.refs_12_), channel_id=1, source_target_pairs={{0,7},{1,0},{2,1},{3,2},{4,3},{5,4},{6,5},{7,6},{8,15},{9,8},{10,9... | collective-permute-start | bytes 786440 | tf_op jit(solution)/shard_map/ppermute | solution.py:475
  119.6 1.9 %collective-permute-done.5.refs_4_ = bf16[256,512]{1,0:T(8,128)(2,1)S(1)} collective-permute-done((bf16[256,512]{1,0:T(8,128)(2,1)S(1)}, bf16[256,512]{1,0:T(8,128)(2,1)S(1)}, u32[]{:S(2)}, u32[]{:S(2)}) %collective-permute-start.5) | collective-permute-done | bytes 262176 | tf_op jit(solution)/shard_map/ppermute | solution.py:475
  121.5 3.7 %collective-permute-start.7 = (bf16[256,512]{1,0:T(8,128)(2,1)S(1)}, bf16[256,512]{1,0:T(8,128)(2,1)S(1)}, u32[]{:S(2)}, u32[]{:S(2)}) collective-permute-start(bf16[256,512]{1,0:T(8,128)(2,1)S(1)} %collective-permute-done.5.refs_4_), channel_id=1, source_target_pairs={{0,7},{1,0},{2,1},{3,2},{4,3},{5,4},{6,5},{7,6},{8,15},{9,8},{10,9... | collective-permute-start | bytes 786440 | tf_op jit(solution)/shard_map/ppermute | solution.py:475
  125.2 0.0 collective-permute-done.11.refs_11_
  125.2 0.0 collective-permute-start.13
  125.2 1.1 collective-permute-done.6.refs_5_
  126.3 0.0 collective-permute-start.8
  126.3 0.8 collective-permute-done.14.refs_14_
  127.2 3.7 %collective-permute-start.15 = (bf16[256,512]{1,0:T(8,128)(2,1)S(1)}, bf16[256,512]{1,0:T(8,128)(2,1)}, u32[]{:S(2)}, u32[]{:S(2)}) collective-permute-start(bf16[256,512]{1,0:T(8,128)(2,1)S(1)} %collective-permute-done.14.refs_14_), channel_id=1, source_target_pairs={{0,7},{1,0},{2,1},{3,2},{4,3},{5,4},{6,5},{7,6},{8,15},{9,8},{10,9... | collective-permute-start | bytes 786440 | tf_op jit(solution)/shard_map/ppermute | solution.py:475
  130.8 1.9 %collective-permute-done.7.refs_6_ = bf16[256,512]{1,0:T(8,128)(2,1)S(1)} collective-permute-done((bf16[256,512]{1,0:T(8,128)(2,1)S(1)}, bf16[256,512]{1,0:T(8,128)(2,1)S(1)}, u32[]{:S(2)}, u32[]{:S(2)}) %collective-permute-start.7) | collective-permute-done | bytes 262176 | tf_op jit(solution)/shard_map/ppermute | solution.py:475
  132.8 3.0 %collective-permute-done.13.refs_13_ = bf16[256,512]{1,0:T(8,128)(2,1)} collective-permute-done((bf16[256,512]{1,0:T(8,128)(2,1)S(1)}, bf16[256,512]{1,0:T(8,128)(2,1)}, u32[]{:S(2)}, u32[]{:S(2)}) %collective-permute-start.13) | collective-permute-done | bytes 262176 | tf_op jit(solution)/shard_map/ppermute | solution.py:475
  135.8 3.1 %collective-permute-done.8.refs_7_ = bf16[256,512]{1,0:T(8,128)(2,1)} collective-permute-done((bf16[256,512]{1,0:T(8,128)(2,1)S(1)}, bf16[256,512]{1,0:T(8,128)(2,1)}, u32[]{:S(2)}, u32[]{:S(2)}) %collective-permute-start.8) | collective-permute-done | bytes 262176 | tf_op jit(solution)/shard_map/ppermute | solution.py:475
  138.9 0.0 collective-permute-done.15.refs_15_
  138.9 0.0 copy-done.6
  138.9 0.0 copy-done.9
  138.9 0.0 copy-done.10
  138.9 0.0 copy-done.11
  138.9 0.0 copy-done.12
  139.0 0.0 copy-done.13
  139.0 9.4 %project.1 = bf16[512,1024]{1,0:T(8,128)(2,1)} custom-call(s32[1]{0:T(128)} %bitcast.place_ref, bf16[256,512]{1,0:T(8,128)(2,1)S(1)} %attend.2.refs_0_, bf16[256,512]{1,0:T(8,128)(2,1)S(1)} %collective-permute-done.2.refs_1_, bf16[256,512]{1,0:T(8,128)(2,1)S(1)} %collective-permute-done.3.refs_2_, bf16[256,512]{1,0:T(8,128)(2,1)S(1)} %collective-permute-done.4.refs_3_, ...), custom_call_target="tpu_custom_call" | custom-call | flops 4294967296 | bytes 8388608 | tf_op jit(solution)/shard_map/project/pallas_call | solution.py:431
  (6 shorter events, 0.0 us)
Async XLA Ops:
  6.5 8.5 %collective-permute-start = (bf16[512,256]{1,0:T(8,128)(2,1)}, bf16[512,256]{1,0:T(8,128)(2,1)S(1)}, u32[]{:S(2)}, u32[]{:S(2)}) collective-permute-start(bf16[512,256]{1,0:T(8,128)(2,1)} %param.18), channel_id=1, source_target_pairs={{0,0},{1,33},{2,66},{3,99},{4,132},{5,165},{6,198},{7,231},{8,8},{... | collective-permute-start | bytes 786440 | tf_op jit(solution)/shard_map/ppermute | solution.py:461
  14.9 9.0 %copy-start = (f32[336,128]{1,0:T(8,128)S(1)}, f32[336,128]{1,0:T(8,128)}, u32[]{:S(2)}) copy-start(f32[336,128]{1,0:T(8,128)} %constant.11.clone.table_ref.tables) | copy-start | bytes 516100
  14.9 9.0 %copy-start.1 = (bf16[512,512]{1,0:T(8,128)(2,1)S(1)}, bf16[512,512]{1,0:T(8,128)(2,1)}, u32[]{:S(2)}) copy-start(bf16[512,512]{1,0:T(8,128)(2,1)} %query_ref) | copy-start | bytes 1572868
  14.9 9.0 %copy-start.2 = (bf16[512,128]{1,0:T(8,128)(2,1)S(1)}, bf16[512,128]{1,0:T(8,128)(2,1)}, u32[]{:S(2)}) copy-start(bf16[512,128]{1,0:T(8,128)(2,1)} %key_ref) | copy-start | bytes 393220
  15.0 9.0 %copy-start.3 = (s32[64,32]{0,1:T(8,128)S(1)}, s32[64,32]{0,1:T(8,128)}, u32[]{:S(2)}) copy-start(s32[64,32]{0,1:T(8,128)} %param.17) | copy-start | bytes 24580
  15.0 9.0 %copy-start.4 = (s32[64]{0:T(128)S(1)}, s32[64]{0:T(128)}, u32[]{:S(2)}) copy-start(s32[64]{0:T(128)} %seats_ref.1) | copy-start | bytes 772
  15.0 9.0 %copy-start.5 = (s32[64]{0:T(128)S(1)}, s32[64]{0:T(128)}, u32[]{:S(2)}) copy-start(s32[64]{0:T(128)} %lengths_ref.1) | copy-start | bytes 772
  15.0 59.6 %copy-start.7 = (bf16[512,128]{1,0:T(8,128)(2,1)S(1)}, bf16[512,128]{1,0:T(8,128)(2,1)}, u32[]{:S(2)}) copy-start(bf16[512,128]{1,0:T(8,128)(2,1)} %turn_val_ref.3) | copy-start | bytes 393220
  15.0 59.5 %all-to-all-start = ((bf16[64,2,128,128]{3,2,1,0:T(8,128)(2,1)}), bf16[64,2,128,128]{3,2,1,0:T(8,128)(2,1)}, u32[]{:S(2)}, u32[]{:S(2)}) async-start(bf16[64,2,128,128]{3,2,1,0:T(8,128)(2,1)} %send_blocks.1), calls=%async_computation | async-start | bytes 8388608 | tf_op jit(solution)/shard_map/all_to_all | solution.py:539
  23.2 115.7 %all-gather.3.cloned.1.call-start = ((), (), s32[]{:S(2)}) async-start(), calls=%async_computation.1 | async-start | bytes 8650752 | tf_op jit(solution)/shard_map/all_gather | solution.py:548
  23.2 3.1 %collective-permute-start.1 = (bf16[512,256]{1,0:T(8,128)(2,1)S(1)}, bf16[512,256]{1,0:T(8,128)(2,1)S(1)}, u32[]{:S(2)}, u32[]{:S(2)}) collective-permute-start(bf16[512,256]{1,0:T(8,128)(2,1)S(1)} %collective-permute-done), channel_id=1, source_target_pairs={{0,0},{33,32},{66,64},{99,96},{132,128},{165,160},{198,192},{231,2... | collective-permute-start | bytes 786440 | tf_op jit(solution)/shard_map/ppermute | solution.py:470
  26.4 48.2 %copy-start.8 = (bf16[512,256]{1,0:T(8,128)(2,1)}, bf16[512,256]{1,0:T(8,128)(2,1)S(1)}, u32[]{:S(2)}) copy-start(bf16[512,256]{1,0:T(8,128)(2,1)S(1)} %collective-permute-done.1) | copy-start | bytes 786436
  79.5 16.1 %collective-permute-start.2 = (bf16[256,512]{1,0:T(8,128)(2,1)S(1)}, bf16[256,512]{1,0:T(8,128)(2,1)S(1)}, u32[]{:S(2)}, u32[]{:S(2)}) collective-permute-start(bf16[256,512]{1,0:T(8,128)(2,1)S(1)} %attend.2.refs_0_), channel_id=1, source_target_pairs={{0,1},{1,2},{2,3},{3,4},{4,5},{5,6},{6,7},{7,0},{8,9},{9,10},{10,1... | collective-permute-start | bytes 786440 | tf_op jit(solution)/shard_map/ppermute | solution.py:475
  84.2 11.5 %collective-permute-start.3 = (bf16[256,512]{1,0:T(8,128)(2,1)S(1)}, bf16[256,512]{1,0:T(8,128)(2,1)S(1)}, u32[]{:S(2)}, u32[]{:S(2)}) collective-permute-start(bf16[256,512]{1,0:T(8,128)(2,1)S(1)} %attend.2.refs_0_), channel_id=1, source_target_pairs={{0,7},{1,0},{2,1},{3,2},{4,3},{5,4},{6,5},{7,6},{8,15},{9,8},{10,9... | collective-permute-start | bytes 786440 | tf_op jit(solution)/shard_map/ppermute | solution.py:475
  95.4 43.5 %copy-start.6 = (bf16[256,512]{1,0:T(8,128)(2,1)}, bf16[256,512]{1,0:T(8,128)(2,1)S(1)}, u32[]{:S(2)}) copy-start(bf16[256,512]{1,0:T(8,128)(2,1)S(1)} %attend.3.refs_8_) | copy-start | bytes 786436
  95.7 9.9 %collective-permute-start.10 = (bf16[256,512]{1,0:T(8,128)(2,1)S(1)}, bf16[256,512]{1,0:T(8,128)(2,1)S(1)}, u32[]{:S(2)}, u32[]{:S(2)}) collective-permute-start(bf16[256,512]{1,0:T(8,128)(2,1)S(1)} %attend.3.refs_8_), channel_id=1, source_target_pairs={{0,7},{1,0},{2,1},{3,2},{4,3},{5,4},{6,5},{7,6},{8,15},{9,8},{10,9... | collective-permute-start | bytes 786440 | tf_op jit(solution)/shard_map/ppermute | solution.py:475
  99.3 10.2 %collective-permute-start.9 = (bf16[256,512]{1,0:T(8,128)(2,1)S(1)}, bf16[256,512]{1,0:T(8,128)(2,1)S(1)}, u32[]{:S(2)}, u32[]{:S(2)}) collective-permute-start(bf16[256,512]{1,0:T(8,128)(2,1)S(1)} %attend.3.refs_8_), channel_id=1, source_target_pairs={{0,1},{1,2},{2,3},{3,4},{4,5},{5,6},{6,7},{7,0},{8,9},{9,10},{10,1... | collective-permute-start | bytes 786440 | tf_op jit(solution)/shard_map/ppermute | solution.py:475
  99.3 15.8 %collective-permute-start.4 = (bf16[256,512]{1,0:T(8,128)(2,1)S(1)}, bf16[256,512]{1,0:T(8,128)(2,1)S(1)}, u32[]{:S(2)}, u32[]{:S(2)}) collective-permute-start(bf16[256,512]{1,0:T(8,128)(2,1)S(1)} %collective-permute-done.2.refs_1_), channel_id=1, source_target_pairs={{0,1},{1,2},{2,3},{3,4},{4,5},{5,6},{6,7},{7,0},{8,9},{9,10},{10,1... | collective-permute-start | bytes 786440 | tf_op jit(solution)/shard_map/ppermute | solution.py:475
  105.6 33.4 %copy-start.9 = (bf16[256,512]{1,0:T(8,128)(2,1)}, bf16[256,512]{1,0:T(8,128)(2,1)S(1)}, u32[]{:S(2)}) copy-start(bf16[256,512]{1,0:T(8,128)(2,1)S(1)} %collective-permute-done.10.refs_10_) | copy-start | bytes 786436
  105.6 10.3 %collective-permute-start.12 = (bf16[256,512]{1,0:T(8,128)(2,1)S(1)}, bf16[256,512]{1,0:T(8,128)(2,1)S(1)}, u32[]{:S(2)}, u32[]{:S(2)}) collective-permute-start(bf16[256,512]{1,0:T(8,128)(2,1)S(1)} %collective-permute-done.10.refs_10_), channel_id=1, source_target_pairs={{0,7},{1,0},{2,1},{3,2},{4,3},{5,4},{6,5},{7,6},{8,15},{9,8},{10,9... | collective-permute-start | bytes 786440 | tf_op jit(solution)/shard_map/ppermute | solution.py:475
  109.3 12.3 %collective-permute-start.5 = (bf16[256,512]{1,0:T(8,128)(2,1)S(1)}, bf16[256,512]{1,0:T(8,128)(2,1)S(1)}, u32[]{:S(2)}, u32[]{:S(2)}) collective-permute-start(bf16[256,512]{1,0:T(8,128)(2,1)S(1)} %collective-permute-done.3.refs_2_), channel_id=1, source_target_pairs={{0,7},{1,0},{2,1},{3,2},{4,3},{5,4},{6,5},{7,6},{8,15},{9,8},{10,9... | collective-permute-start | bytes 786440 | tf_op jit(solution)/shard_map/ppermute | solution.py:475
  109.5 29.5 %copy-start.10 = (bf16[256,512]{1,0:T(8,128)(2,1)}, bf16[256,512]{1,0:T(8,128)(2,1)S(1)}, u32[]{:S(2)}) copy-start(bf16[256,512]{1,0:T(8,128)(2,1)S(1)} %collective-permute-done.9.refs_9_) | copy-start | bytes 786436
  109.5 15.8 %collective-permute-start.11 = (bf16[256,512]{1,0:T(8,128)(2,1)S(1)}, bf16[256,512]{1,0:T(8,128)(2,1)S(1)}, u32[]{:S(2)}, u32[]{:S(2)}) collective-permute-start(bf16[256,512]{1,0:T(8,128)(2,1)S(1)} %collective-permute-done.9.refs_9_), channel_id=1, source_target_pairs={{0,1},{1,2},{2,3},{3,4},{4,5},{5,6},{6,7},{7,0},{8,9},{9,10},{10,1... | collective-permute-start | bytes 786440 | tf_op jit(solution)/shard_map/ppermute | solution.py:475
  115.1 11.2 %collective-permute-start.6 = (bf16[256,512]{1,0:T(8,128)(2,1)S(1)}, bf16[256,512]{1,0:T(8,128)(2,1)S(1)}, u32[]{:S(2)}, u32[]{:S(2)}) collective-permute-start(bf16[256,512]{1,0:T(8,128)(2,1)S(1)} %collective-permute-done.4.refs_3_), channel_id=1, source_target_pairs={{0,1},{1,2},{2,3},{3,4},{4,5},{5,6},{6,7},{7,0},{8,9},{9,10},{10,1... | collective-permute-start | bytes 786440 | tf_op jit(solution)/shard_map/ppermute | solution.py:475
  115.9 23.0 %copy-start.11 = (bf16[256,512]{1,0:T(8,128)(2,1)}, bf16[256,512]{1,0:T(8,128)(2,1)S(1)}, u32[]{:S(2)}) copy-start(bf16[256,512]{1,0:T(8,128)(2,1)S(1)} %collective-permute-done.12.refs_12_) | copy-start | bytes 786436
  115.9 11.2 %collective-permute-start.14 = (bf16[256,512]{1,0:T(8,128)(2,1)S(1)}, bf16[256,512]{1,0:T(8,128)(2,1)S(1)}, u32[]{:S(2)}, u32[]{:S(2)}) collective-permute-start(bf16[256,512]{1,0:T(8,128)(2,1)S(1)} %collective-permute-done.12.refs_12_), channel_id=1, source_target_pairs={{0,7},{1,0},{2,1},{3,2},{4,3},{5,4},{6,5},{7,6},{8,15},{9,8},{10,9... | collective-permute-start | bytes 786440 | tf_op jit(solution)/shard_map/ppermute | solution.py:475
  121.5 11.2 %collective-permute-start.7 = (bf16[256,512]{1,0:T(8,128)(2,1)S(1)}, bf16[256,512]{1,0:T(8,128)(2,1)S(1)}, u32[]{:S(2)}, u32[]{:S(2)}) collective-permute-start(bf16[256,512]{1,0:T(8,128)(2,1)S(1)} %collective-permute-done.5.refs_4_), channel_id=1, source_target_pairs={{0,7},{1,0},{2,1},{3,2},{4,3},{5,4},{6,5},{7,6},{8,15},{9,8},{10,9... | collective-permute-start | bytes 786440 | tf_op jit(solution)/shard_map/ppermute | solution.py:475
  125.2 13.7 %copy-start.12 = (bf16[256,512]{1,0:T(8,128)(2,1)}, bf16[256,512]{1,0:T(8,128)(2,1)S(1)}, u32[]{:S(2)}) copy-start(bf16[256,512]{1,0:T(8,128)(2,1)S(1)} %collective-permute-done.11.refs_11_) | copy-start | bytes 786436
  125.2 10.6 %collective-permute-start.13 = (bf16[256,512]{1,0:T(8,128)(2,1)S(1)}, bf16[256,512]{1,0:T(8,128)(2,1)}, u32[]{:S(2)}, u32[]{:S(2)}) collective-permute-start(bf16[256,512]{1,0:T(8,128)(2,1)S(1)} %collective-permute-done.11.refs_11_), channel_id=1, source_target_pairs={{0,1},{1,2},{2,3},{3,4},{4,5},{5,6},{6,7},{7,0},{8,9},{9,10},{10,1... | collective-permute-start | bytes 786440 | tf_op jit(solution)/shard_map/ppermute | solution.py:475
  126.3 12.6 %collective-permute-start.8 = (bf16[256,512]{1,0:T(8,128)(2,1)S(1)}, bf16[256,512]{1,0:T(8,128)(2,1)}, u32[]{:S(2)}, u32[]{:S(2)}) collective-permute-start(bf16[256,512]{1,0:T(8,128)(2,1)S(1)} %collective-permute-done.6.refs_5_), channel_id=1, source_target_pairs={{0,1},{1,2},{2,3},{3,4},{4,5},{5,6},{6,7},{7,0},{8,9},{9,10},{10,1... | collective-permute-start | bytes 786440 | tf_op jit(solution)/shard_map/ppermute | solution.py:475
  127.2 11.8 %copy-start.13 = (bf16[256,512]{1,0:T(8,128)(2,1)}, bf16[256,512]{1,0:T(8,128)(2,1)S(1)}, u32[]{:S(2)}) copy-start(bf16[256,512]{1,0:T(8,128)(2,1)S(1)} %collective-permute-done.14.refs_14_) | copy-start | bytes 786436
  127.2 11.8 %collective-permute-start.15 = (bf16[256,512]{1,0:T(8,128)(2,1)S(1)}, bf16[256,512]{1,0:T(8,128)(2,1)}, u32[]{:S(2)}, u32[]{:S(2)}) collective-permute-start(bf16[256,512]{1,0:T(8,128)(2,1)S(1)} %collective-permute-done.14.refs_14_), channel_id=1, source_target_pairs={{0,7},{1,0},{2,1},{3,2},{4,3},{5,4},{6,5},{7,6},{8,15},{9,8},{10,9... | collective-permute-start | bytes 786440 | tf_op jit(solution)/shard_map/ppermute | solution.py:475
Sparse Core Ops, SparseCore 0:
  74.7 62.7 all-gather.2

commit v4 on v3

--- a/solution.py
+++ b/solution.py
@@ -50,30 +50,25 @@
 
 
 def send_kernel(
-    base_count,
     place_ref,
     seats_ref,
     lengths_ref,
     map_ref,
-    table_ref,
     keys_ref,
     vals_ref,
     out_ref,
     held,
-    tables,
     plan,
     plan_scalar,
     in_sems,
     out_sems,
-    other_sems,
+    plan_sem,
 ):
     count = held.shape[0]
     blocks_here, block_rows = keys_ref.shape[:2]
     block_count, sessions = map_ref.shape
     shift = blocks_here.bit_length() - 1
     lanes = plan.shape[1]
-    get_tables = pltpu.make_async_copy(table_ref, tables, other_sems.at[0])
-    get_tables.start()
 
     lengths = lengths_ref[...].astype(jnp.float32)
     block = lax.broadcasted_iota(jnp.int32, (block_count, sessions), 0)
@@ -111,11 +106,11 @@
     )
     even = lax.broadcasted_iota(jnp.int32, (1, lanes), 1) % 2 == 0
     plan[...] = jnp.where(even, first, pltpu.roll(second, 1, 1)).astype(jnp.int32)
-    to_scalar = pltpu.make_async_copy(plan, plan_scalar, other_sems.at[1])
+    to_scalar = pltpu.make_async_copy(plan, plan_scalar, plan_sem.at[0])
     to_scalar.start()
     to_scalar.wait()
 
-    @pl.loop(0, count)
+    @pl.loop(0, count, unroll=4)
     def _(i):
         code = plan_scalar[0, i]
 
@@ -125,52 +120,40 @@
             pltpu.make_async_copy(keys_ref.at[slot], held.at[i, 0], in_sems.at[i]).start()
             pltpu.make_async_copy(vals_ref.at[slot], held.at[i, 1], in_sems.at[i]).start()
 
-    get_tables.wait()
-    row_cos, row_sin, base_cos, base_sin = table_rows(block_rows, base_count)
-
-    @pl.loop(0, count)
+    @pl.loop(0, count, unroll=4)
     def _(i):
         code = plan_scalar[0, i]
 
         @pl.when(code >= 0)
         def _():
             pltpu.make_async_copy(held.at[i], held.at[i], in_sems.at[i]).wait()
-            position = code >> shift
-            cosine, sine = add_angles(
-                tables[row_cos, :],
-                tables[row_sin, :],
-                tables[pl.ds(base_cos + position, 1), :],
-                tables[pl.ds(base_sin + position, 1), :],
-            )
-            held[i, 0] = rope(held[i, 0].astype(jnp.float32), cosine, sine).astype(jnp.bfloat16)
             pltpu.make_async_copy(held.at[i], out_ref.at[i], out_sems.at[i]).start()
 
-    @pl.loop(0, count)
+    @pl.loop(0, count, unroll=4)
     def _(i):
         @pl.when(plan_scalar[0, i] >= 0)
         def _():
             pltpu.make_async_copy(held.at[i], out_ref.at[i], out_sems.at[i]).wait()
 
 
-def send_blocks(place, seats, lengths, map_t, table, base_count, pool_keys, pool_values, count):
+def send_blocks(place, seats, lengths, map_t, pool_keys, pool_values, count):
     block_shape = pool_keys.shape[1:]
     return pl.pallas_call(
-        functools.partial(send_kernel, base_count),
+        send_kernel,
         out_shape=jax.ShapeDtypeStruct((count, 2) + block_shape, pool_keys.dtype),
-        in_specs=[SMEM] + [VMEM] * 3 + [ANY] * 3,
+        in_specs=[SMEM] + [VMEM] * 3 + [ANY] * 2,
         out_specs=ANY,
         scratch_shapes=[
             pltpu.VMEM((count, 2) + block_shape, pool_keys.dtype),
-            pltpu.VMEM(table.shape, jnp.float32),
             pltpu.VMEM((1, 128), jnp.int32),
             pltpu.SMEM((1, 128), jnp.int32),
             pltpu.SemaphoreType.DMA((count,)),
             pltpu.SemaphoreType.DMA((count,)),
-            pltpu.SemaphoreType.DMA((2,)),
+            pltpu.SemaphoreType.DMA((1,)),
         ],
         compiler_params=pltpu.CompilerParams(vmem_limit_bytes=60 * MIB),
         name="send_blocks",
-    )(place, seats[None, :], lengths[None, :], map_t, table, pool_keys, pool_values)
+    )(place, seats[None, :], lengths[None, :], map_t, pool_keys, pool_values)
 
 
 def prepare_kernel(
@@ -275,14 +258,17 @@
 
 def attention_kernel(
     seat,
+    base_count,
     index_ref,
     length_ref,
     query_ref,
     turn_key_ref,
     turn_val_ref,
+    tables,
     arrived_ref,
     out_ref,
     blocks,
+    roped,
     top_ref,
     acc_ref,
     sems,
@@ -293,6 +279,7 @@
     length = length_ref[seat]
     chunks = pl.cdiv(length, chunk_rows)
     full = length // chunk_rows
+    row_cos, row_sin, base_cos, base_sin = table_rows(block_rows, base_count)
 
     def copy(j):
         return pltpu.make_async_copy(arrived_ref.at[index_ref[seat, j]], blocks.at[j], sems.at[j])
@@ -329,7 +316,16 @@
             for i in range(4):
                 copy(first + j + i).wait()
 
-        keys = blocks[pl.ds(first, CHUNK_BLOCKS), 0].reshape(chunk_rows, head_dim)
+        for i in range(CHUNK_BLOCKS):
+            cosine, sine = add_angles(
+                tables[row_cos, :],
+                tables[row_sin, :],
+                tables[pl.ds(base_cos + first + i, 1), :],
+                tables[pl.ds(base_sin + first + i, 1), :],
+            )
+            key = rope(blocks[first + i, 0].astype(jnp.float32), cosine, sine)
+            roped[i * block_rows : (i + 1) * block_rows, :] = key.astype(jnp.bfloat16)
+        keys = roped[...]
         vals = with_ones(blocks[pl.ds(first, CHUNK_BLOCKS), 1].reshape(chunk_rows, head_dim))
         seen = [scores(h, keys) for h in range(heads)]
         if masked:
@@ -360,18 +356,19 @@
         ).astype(jnp.bfloat16)
 
 
-def attend(seat, recv_index, lengths, query, turn_key, turn_val, arrived):
+def attend(seat, base_count, recv_index, lengths, query, turn_key, turn_val, table, arrived):
     _, heads, turn_len, head_dim = query.shape
     block_rows = arrived.shape[2]
     block_count = recv_index.shape[1]
     keys_seen = block_count * block_rows + turn_len
     return pl.pallas_call(
-        functools.partial(attention_kernel, seat),
+        functools.partial(attention_kernel, seat, base_count),
         out_shape=jax.ShapeDtypeStruct((turn_len, heads * head_dim), jnp.bfloat16),
-        in_specs=[SMEM] * 2 + [VMEM] * 3 + [ANY],
+        in_specs=[SMEM] * 2 + [VMEM] * 4 + [ANY],
         out_specs=VMEM,
         scratch_shapes=[
             pltpu.VMEM((block_count, 2, block_rows, head_dim), jnp.bfloat16),
+            pltpu.VMEM((CHUNK_BLOCKS * block_rows, head_dim), jnp.bfloat16),
             pltpu.VMEM((heads, turn_len, 1), jnp.float32),
             pltpu.VMEM((heads, turn_len, 2 * head_dim), jnp.float32),
             pltpu.SemaphoreType.DMA((block_count,)),
@@ -383,7 +380,7 @@
             transcendentals=heads * turn_len * keys_seen,
         ),
         name="attend",
-    )(recv_index, lengths, query, turn_key, turn_val, arrived)
+    )(recv_index, lengths, query, turn_key, turn_val, table, arrived)
 
 
 def project_kernel(distances, started, place_ref, *refs):
@@ -449,7 +446,7 @@
 
 
 def weight_place(plane, tp, rest, pieces):
-    return (plane ^ tp) * pieces + rest
+    return ((plane ^ tp) * pieces + rest) ^ ((tp & 1) * (pieces // 2))
 
 
 def spread_weights(out_weight, pieces):
@@ -529,8 +526,6 @@
         seat_session,
         history_len,
         map_t,
-        table,
-        base_count,
         pool_keys,
         pool_values,
         pooled_count * capacity,
@@ -549,7 +544,9 @@
 
     gathered = []
     for seat in range(per_owner):
-        attended = attend(seat, recv_index, own_lengths, queries, new_keys, turn_value, arrived)
+        attended = attend(
+            seat, base_count, recv_index, own_lengths, queries, new_keys, turn_value, table, arrived
+        )
         if gathered:
             attended, *_ = lax.optimization_barrier((attended, *gathered[-1][1:3]))
         ring, distances = gather_ring(attended, seat % 2 == 0)

time: 157 us -> 156 us (level)
  no operation moved by 1% of the time
where the time goes in v4:
time: 156 us; the launch traced here: 153 us
  waiting for transfers between devices  70.5 us (45%)
  starting transfers between devices  41.6 us (27%)
  Pallas kernels  27.6 us (18%)
  between operations  13.7 us (9%)
    all_to_all x1, waiting for transfers between devices, local(): lax.all_to_all(sent, 'pool', split_axis=0, concat_axis=0, tiled=True)  48.2 us
    ppermute x14, starting transfers between devices, shift_tp(): lax.ppermute(values, 'tp', [(i, (i + step) % count) for i in range(count)])  31.5 us
    ppermute x14, waiting for transfers between devices, shift_tp(): lax.ppermute(values, 'tp', [(i, (i + step) % count) for i in range(count)])  22.3 us
    pallas_call x2, Pallas kernels, attend(): pl.pallas_call(functools.partial(attention_kernel, seat, base_count), out...  10.8 us
    pallas_call x1, Pallas kernels, project(): pl.pallas_call(functools.partial(project_kernel, distances, before is not...  9.47 us
    all_to_all x1, starting transfers between devices, local(): lax.all_to_all(sent, 'pool', split_axis=0, concat_axis=0, tiled=True)  7.79 us
    pallas_call x1, Pallas kernels, send_blocks(): pl.pallas_call(send_kernel, out_shape=jax.ShapeDtypeStruct((count, 2) + b...  4.91 us
  transfers between devices with their start and end apart: 18, of which 12 were waited for; matrix products, arithmetic and copies ran while one was open for 0% of the time, Pallas kernels for 12%

profile of v4, /device:TPU:2, one launch (start us, length us, event | category | flops | bytes accessed | tf_op | source)
XLA Modules:
  0.0 153.4 jit_solution(13158358789227820593)
XLA Ops:
  6.5 1.6 %collective-permute-start = (bf16[512,256]{1,0:T(8,128)(2,1)}, bf16[512,256]{1,0:T(8,128)(2,1)S(1)}, u32[]{:S(2)}, u32[]{:S(2)}) collective-permute-start(bf16[512,256]{1,0:T(8,128)(2,1)} %param.18), channel_id=1, source_target_pairs={{0,0},{1,49},{2,66},{3,115},{4,132},{5,181},{6,198},{7,247},{8,8},... | collective-permute-start | bytes 786440 | tf_op jit(solution)/shard_map/ppermute | solution.py:458
  8.1 4.9 %send_blocks.1 = bf16[64,2,128,128]{3,2,1,0:T(8,128)(2,1)} custom-call(s32[1]{0:T(128)} %bitcast.1.place_ref, s32[1,64]{1,0:T(1,128)} %bitcast.8, s32[1,64]{1,0:T(1,128)} %bitcast.9, s32[32,64]{1,0:T(8,128)} %bitcast.6, bf16[64,128,128]{2,1,0:T(8,128)(2,1)} %keys_ref.1, bf16[64,128,128]{2,1,0:T(8,128)(2,1)} %vals_ref.1), custom_call_target="tpu_custom_call" | custom-call | tf_op jit(solution)/shard_map/send_blocks/pallas_call | solution.py:141
  13.1 0.0 copy-start
  13.1 0.0 copy-start.1
  13.1 0.0 copy-start.2
  13.1 0.0 copy-start.3
  13.1 0.0 copy-start.4
  13.1 0.0 copy-start.5
  13.1 0.0 copy-start.7
  13.1 0.0 collective-permute-done
  13.1 7.8 %all-to-all-start = ((bf16[64,2,128,128]{3,2,1,0:T(8,128)(2,1)}), bf16[64,2,128,128]{3,2,1,0:T(8,128)(2,1)}, u32[]{:S(2)}, u32[]{:S(2)}) async-start(bf16[64,2,128,128]{3,2,1,0:T(8,128)(2,1)} %send_blocks.1), calls=%async_computation | async-start | bytes 8388608 | tf_op jit(solution)/shard_map/all_to_all | solution.py:534
  20.9 0.0 all-gather.3.cloned.1.call-start
  21.0 0.7 collective-permute-start.1
  21.7 0.0 copy-done
  21.7 0.0 copy-done.1
  21.7 0.0 copy-done.2
  21.7 0.0 copy-done.3
  21.7 0.0 copy-done.4
  21.7 0.0 copy-done.5
  21.7 2.4 %prepare_turn.1 = (s32[2,32]{1,0:T(2,128)S(1)}, s32[2]{0:T(128)S(1)}, bf16[2,4,256,128]{3,2,1,0:T(8,128)(2,1)S(1)}, bf16[2,256,128]{2,1,0:T(8,128)(2,1)S(1)}) custom-call(s32[1]{0:T(128)} %bitcast.1.place_ref, s32[64]{0:T(128)S(1)} %copy-done.4, s32[64]{0:T(128)S(1)} %copy-done.5, s32[32,64]{1,0:T(8,128)S(1)} %bitcast.7, f32[336,128]{1,0:T(8,128)S(1)} %copy-done.1, ...), custom_call_target="tpu_custom_call" | custom-call | tf_op jit(solution)/shard_map/prepare_turn/pallas_call | solution.py:237
  24.1 0.0 collective-permute-done.1
  24.1 0.0 copy-start.8
  24.2 48.2 %all-to-all-done.arrived_ref = bf16[64,2,128,128]{3,2,1,0:T(8,128)(2,1)} async-done(((bf16[64,2,128,128]{3,2,1,0:T(8,128)(2,1)}), bf16[64,2,128,128]{3,2,1,0:T(8,128)(2,1)}, u32[]{:S(2)}, u32[]{:S(2)}) %all-to-all-start) | async-done | bytes 4194336 | tf_op jit(solution)/shard_map/all_to_all | solution.py:534
  72.3 0.0 copy-done.8
  72.3 0.0 all-gather.3.cloned.1.call-update
  72.3 0.0 copy-done.7
  72.4 5.5 %attend.2.refs_0_ = bf16[256,512]{1,0:T(8,128)(2,1)S(1)} custom-call(s32[2,32]{1,0:T(2,128)S(1)} %get-tuple-element.20.index_ref, s32[2]{0:T(128)S(1)} %get-tuple-element.21.length_ref, bf16[2,4,256,128]{3,2,1,0:T(8,128)(2,1)S(1)} %get-tuple-element.24.query_ref, bf16[2,256,128]{2,1,0:T(8,128)(2,1)S(1)} %get-tuple-element.25.turn_key_ref, ...), custom_call_target="tpu_custom_call" | custom-call | flops 2281701376 | bytes 2097152 | tf_op jit(solution)/shard_map/attend/pallas_call | solution.py:364
  77.9 6.3 %collective-permute-start.2 = (bf16[256,512]{1,0:T(8,128)(2,1)S(1)}, bf16[256,512]{1,0:T(8,128)(2,1)S(1)}, u32[]{:S(2)}, u32[]{:S(2)}) collective-permute-start(bf16[256,512]{1,0:T(8,128)(2,1)S(1)} %attend.2.refs_0_), channel_id=1, source_target_pairs={{0,1},{1,2},{2,3},{3,4},{4,5},{5,6},{6,7},{7,0},{8,9},{9,10},{10,1... | collective-permute-start | bytes 786440 | tf_op jit(solution)/shard_map/ppermute | solution.py:472
  84.2 6.0 %collective-permute-start.3 = (bf16[256,512]{1,0:T(8,128)(2,1)S(1)}, bf16[256,512]{1,0:T(8,128)(2,1)S(1)}, u32[]{:S(2)}, u32[]{:S(2)}) collective-permute-start(bf16[256,512]{1,0:T(8,128)(2,1)S(1)} %attend.2.refs_0_), channel_id=1, source_target_pairs={{0,7},{1,0},{2,1},{3,2},{4,3},{5,4},{6,5},{7,6},{8,15},{9,8},{10,9... | collective-permute-start | bytes 786440 | tf_op jit(solution)/shard_map/ppermute | solution.py:472
  90.2 5.3 %attend.3.refs_8_ = bf16[256,512]{1,0:T(8,128)(2,1)S(1)} custom-call(s32[2,32]{1,0:T(2,128)S(1)} %get-tuple-element.20.index_ref, s32[2]{0:T(128)S(1)} %get-tuple-element.21.length_ref, bf16[2,4,256,128]{3,2,1,0:T(8,128)(2,1)S(1)} %get-tuple-element.24.query_ref, bf16[2,256,128]{2,1,0:T(8,128)(2,1)S(1)} %get-tuple-element.25.turn_key_ref, ...), custom_call_target="tpu_custom_call" | custom-call | flops 2281701376 | bytes 2097152 | tf_op jit(solution)/shard_map/attend/pallas_call | solution.py:364
  95.5 0.0 copy-start.6
  95.5 0.6 collective-permute-done.2.refs_1_
  96.1 0.0 collective-permute-done.3.refs_2_
  96.1 3.0 %collective-permute-start.10 = (bf16[256,512]{1,0:T(8,128)(2,1)S(1)}, bf16[256,512]{1,0:T(8,128)(2,1)S(1)}, u32[]{:S(2)}, u32[]{:S(2)}) collective-permute-start(bf16[256,512]{1,0:T(8,128)(2,1)S(1)} %attend.3.refs_8_), channel_id=1, source_target_pairs={{0,7},{1,0},{2,1},{3,2},{4,3},{5,4},{6,5},{7,6},{8,15},{9,8},{10,9... | collective-permute-start | bytes 786440 | tf_op jit(solution)/shard_map/ppermute | solution.py:472
  99.1 0.0 collective-permute-start.9
  99.1 0.0 collective-permute-start.4
  99.1 6.0 %collective-permute-done.10.refs_10_ = bf16[256,512]{1,0:T(8,128)(2,1)S(1)} collective-permute-done((bf16[256,512]{1,0:T(8,128)(2,1)S(1)}, bf16[256,512]{1,0:T(8,128)(2,1)S(1)}, u32[]{:S(2)}, u32[]{:S(2)}) %collective-permute-start.10) | collective-permute-done | bytes 262176 | tf_op jit(solution)/shard_map/ppermute | solution.py:472
  105.1 3.7 %collective-permute-start.12 = (bf16[256,512]{1,0:T(8,128)(2,1)S(1)}, bf16[256,512]{1,0:T(8,128)(2,1)S(1)}, u32[]{:S(2)}, u32[]{:S(2)}) collective-permute-start(bf16[256,512]{1,0:T(8,128)(2,1)S(1)} %collective-permute-done.10.refs_10_), channel_id=1, source_target_pairs={{0,7},{1,0},{2,1},{3,2},{4,3},{5,4},{6,5},{7,6},{8,15},{9,8},{10,9... | collective-permute-start | bytes 786440 | tf_op jit(solution)/shard_map/ppermute | solution.py:472
  108.8 0.0 collective-permute-start.5
  108.9 0.7 collective-permute-done.9.refs_9_
  109.5 1.3 collective-permute-start.11
  110.9 4.3 %collective-permute-done.4.refs_3_ = bf16[256,512]{1,0:T(8,128)(2,1)S(1)} collective-permute-done((bf16[256,512]{1,0:T(8,128)(2,1)S(1)}, bf16[256,512]{1,0:T(8,128)(2,1)S(1)}, u32[]{:S(2)}, u32[]{:S(2)}) %collective-permute-start.4) | collective-permute-done | bytes 262176 | tf_op jit(solution)/shard_map/ppermute | solution.py:472
  115.1 0.0 collective-permute-start.6
  115.1 0.5 collective-permute-done.12.refs_12_
  115.6 3.7 %collective-permute-start.14 = (bf16[256,512]{1,0:T(8,128)(2,1)S(1)}, bf16[256,512]{1,0:T(8,128)(2,1)S(1)}, u32[]{:S(2)}, u32[]{:S(2)}) collective-permute-start(bf16[256,512]{1,0:T(8,128)(2,1)S(1)} %collective-permute-done.12.refs_12_), channel_id=1, source_target_pairs={{0,7},{1,0},{2,1},{3,2},{4,3},{5,4},{6,5},{7,6},{8,15},{9,8},{10,9... | collective-permute-start | bytes 786440 | tf_op jit(solution)/shard_map/ppermute | solution.py:472
  119.3 1.9 %collective-permute-done.5.refs_4_ = bf16[256,512]{1,0:T(8,128)(2,1)S(1)} collective-permute-done((bf16[256,512]{1,0:T(8,128)(2,1)S(1)}, bf16[256,512]{1,0:T(8,128)(2,1)S(1)}, u32[]{:S(2)}, u32[]{:S(2)}) %collective-permute-start.5) | collective-permute-done | bytes 262176 | tf_op jit(solution)/shard_map/ppermute | solution.py:472
  121.2 3.7 %collective-permute-start.7 = (bf16[256,512]{1,0:T(8,128)(2,1)S(1)}, bf16[256,512]{1,0:T(8,128)(2,1)S(1)}, u32[]{:S(2)}, u32[]{:S(2)}) collective-permute-start(bf16[256,512]{1,0:T(8,128)(2,1)S(1)} %collective-permute-done.5.refs_4_), channel_id=1, source_target_pairs={{0,7},{1,0},{2,1},{3,2},{4,3},{5,4},{6,5},{7,6},{8,15},{9,8},{10,9... | collective-permute-start | bytes 786440 | tf_op jit(solution)/shard_map/ppermute | solution.py:472
  124.9 0.0 collective-permute-done.11.refs_11_
  124.9 0.0 collective-permute-start.13
  124.9 0.5 collective-permute-done.6.refs_5_
  125.4 0.0 collective-permute-start.8
  125.4 1.4 collective-permute-done.14.refs_14_
  126.8 3.7 %collective-permute-start.15 = (bf16[256,512]{1,0:T(8,128)(2,1)S(1)}, bf16[256,512]{1,0:T(8,128)(2,1)}, u32[]{:S(2)}, u32[]{:S(2)}) collective-permute-start(bf16[256,512]{1,0:T(8,128)(2,1)S(1)} %collective-permute-done.14.refs_14_), channel_id=1, source_target_pairs={{0,7},{1,0},{2,1},{3,2},{4,3},{5,4},{6,5},{7,6},{8,15},{9,8},{10,9... | collective-permute-start | bytes 786440 | tf_op jit(solution)/shard_map/ppermute | solution.py:472
  130.5 1.9 %collective-permute-done.7.refs_6_ = bf16[256,512]{1,0:T(8,128)(2,1)S(1)} collective-permute-done((bf16[256,512]{1,0:T(8,128)(2,1)S(1)}, bf16[256,512]{1,0:T(8,128)(2,1)S(1)}, u32[]{:S(2)}, u32[]{:S(2)}) %collective-permute-start.7) | collective-permute-done | bytes 262176 | tf_op jit(solution)/shard_map/ppermute | solution.py:472
  132.4 1.7 %collective-permute-done.13.refs_13_ = bf16[256,512]{1,0:T(8,128)(2,1)} collective-permute-done((bf16[256,512]{1,0:T(8,128)(2,1)S(1)}, bf16[256,512]{1,0:T(8,128)(2,1)}, u32[]{:S(2)}, u32[]{:S(2)}) %collective-permute-start.13) | collective-permute-done | bytes 262176 | tf_op jit(solution)/shard_map/ppermute | solution.py:472
  134.2 2.8 %collective-permute-done.8.refs_7_ = bf16[256,512]{1,0:T(8,128)(2,1)} collective-permute-done((bf16[256,512]{1,0:T(8,128)(2,1)S(1)}, bf16[256,512]{1,0:T(8,128)(2,1)}, u32[]{:S(2)}, u32[]{:S(2)}) %collective-permute-start.8) | collective-permute-done | bytes 262176 | tf_op jit(solution)/shard_map/ppermute | solution.py:472
  137.0 0.0 collective-permute-done.15.refs_15_
  137.0 0.0 all-gather.3.cloned.1.call-done
  137.0 0.0 copy-done.9
  137.0 0.0 copy-done.10
  137.0 0.0 copy-done.11
  137.0 0.0 copy-done.12
  137.0 0.0 copy-done.13
  137.0 9.5 %project.1 = bf16[512,1024]{1,0:T(8,128)(2,1)} custom-call(s32[1]{0:T(128)} %bitcast.place_ref, bf16[256,512]{1,0:T(8,128)(2,1)S(1)} %attend.2.refs_0_, bf16[256,512]{1,0:T(8,128)(2,1)S(1)} %collective-permute-done.2.refs_1_, bf16[256,512]{1,0:T(8,128)(2,1)S(1)} %collective-permute-done.3.refs_2_, bf16[256,512]{1,0:T(8,128)(2,1)S(1)} %collective-permute-done.4.refs_3_, ...), custom_call_target="tpu_custom_call" | custom-call | flops 4294967296 | bytes 8388608 | tf_op jit(solution)/shard_map/project/pallas_call | solution.py:428
  (6 shorter events, 0.0 us)
Async XLA Ops:
  6.5 6.6 %collective-permute-start = (bf16[512,256]{1,0:T(8,128)(2,1)}, bf16[512,256]{1,0:T(8,128)(2,1)S(1)}, u32[]{:S(2)}, u32[]{:S(2)}) collective-permute-start(bf16[512,256]{1,0:T(8,128)(2,1)} %param.18), channel_id=1, source_target_pairs={{0,0},{1,49},{2,66},{3,115},{4,132},{5,181},{6,198},{7,247},{8,8},... | collective-permute-start | bytes 786440 | tf_op jit(solution)/shard_map/ppermute | solution.py:458
  13.1 8.6 %copy-start = (bf16[512,512]{1,0:T(8,128)(2,1)S(1)}, bf16[512,512]{1,0:T(8,128)(2,1)}, u32[]{:S(2)}) copy-start(bf16[512,512]{1,0:T(8,128)(2,1)} %query_ref) | copy-start | bytes 1572868
  13.1 8.6 %copy-start.1 = (f32[336,128]{1,0:T(8,128)S(1)}, f32[336,128]{1,0:T(8,128)}, u32[]{:S(2)}) copy-start(f32[336,128]{1,0:T(8,128)} %constant.11.clone.tables) | copy-start | bytes 516100
  13.1 8.6 %copy-start.2 = (bf16[512,128]{1,0:T(8,128)(2,1)S(1)}, bf16[512,128]{1,0:T(8,128)(2,1)}, u32[]{:S(2)}) copy-start(bf16[512,128]{1,0:T(8,128)(2,1)} %key_ref) | copy-start | bytes 393220
  13.1 8.6 %copy-start.3 = (s32[64,32]{0,1:T(8,128)S(1)}, s32[64,32]{0,1:T(8,128)}, u32[]{:S(2)}) copy-start(s32[64,32]{0,1:T(8,128)} %param.17) | copy-start | bytes 24580
  13.1 8.6 %copy-start.4 = (s32[64]{0:T(128)S(1)}, s32[64]{0:T(128)}, u32[]{:S(2)}) copy-start(s32[64]{0:T(128)} %seats_ref.1) | copy-start | bytes 772
  13.1 8.6 %copy-start.5 = (s32[64]{0:T(128)S(1)}, s32[64]{0:T(128)}, u32[]{:S(2)}) copy-start(s32[64]{0:T(128)} %lengths_ref.1) | copy-start | bytes 772
  13.1 59.2 %copy-start.7 = (bf16[512,128]{1,0:T(8,128)(2,1)S(1)}, bf16[512,128]{1,0:T(8,128)(2,1)}, u32[]{:S(2)}) copy-start(bf16[512,128]{1,0:T(8,128)(2,1)} %turn_val_ref.3) | copy-start | bytes 393220
  13.1 59.2 %all-to-all-start = ((bf16[64,2,128,128]{3,2,1,0:T(8,128)(2,1)}), bf16[64,2,128,128]{3,2,1,0:T(8,128)(2,1)}, u32[]{:S(2)}, u32[]{:S(2)}) async-start(bf16[64,2,128,128]{3,2,1,0:T(8,128)(2,1)} %send_blocks.1), calls=%async_computation | async-start | bytes 8388608 | tf_op jit(solution)/shard_map/all_to_all | solution.py:534
  20.9 116.0 %all-gather.3.cloned.1.call-start = ((), (), s32[]{:S(2)}) async-start(), calls=%async_computation.1 | async-start | bytes 8650752 | tf_op jit(solution)/shard_map/all_gather | solution.py:543
  21.0 3.1 %collective-permute-start.1 = (bf16[512,256]{1,0:T(8,128)(2,1)S(1)}, bf16[512,256]{1,0:T(8,128)(2,1)S(1)}, u32[]{:S(2)}, u32[]{:S(2)}) collective-permute-start(bf16[512,256]{1,0:T(8,128)(2,1)S(1)} %collective-permute-done), channel_id=1, source_target_pairs={{0,0},{49,48},{66,64},{115,112},{132,128},{181,176},{198,192},{247... | collective-permute-start | bytes 786440 | tf_op jit(solution)/shard_map/ppermute | solution.py:467
  24.1 48.2 %copy-start.8 = (bf16[512,256]{1,0:T(8,128)(2,1)}, bf16[512,256]{1,0:T(8,128)(2,1)S(1)}, u32[]{:S(2)}) copy-start(bf16[512,256]{1,0:T(8,128)(2,1)S(1)} %collective-permute-done.1) | copy-start | bytes 786436
  77.9 18.2 %collective-permute-start.2 = (bf16[256,512]{1,0:T(8,128)(2,1)S(1)}, bf16[256,512]{1,0:T(8,128)(2,1)S(1)}, u32[]{:S(2)}, u32[]{:S(2)}) collective-permute-start(bf16[256,512]{1,0:T(8,128)(2,1)S(1)} %attend.2.refs_0_), channel_id=1, source_target_pairs={{0,1},{1,2},{2,3},{3,4},{4,5},{5,6},{6,7},{7,0},{8,9},{9,10},{10,1... | collective-permute-start | bytes 786440 | tf_op jit(solution)/shard_map/ppermute | solution.py:472
  84.2 11.9 %collective-permute-start.3 = (bf16[256,512]{1,0:T(8,128)(2,1)S(1)}, bf16[256,512]{1,0:T(8,128)(2,1)S(1)}, u32[]{:S(2)}, u32[]{:S(2)}) collective-permute-start(bf16[256,512]{1,0:T(8,128)(2,1)S(1)} %attend.2.refs_0_), channel_id=1, source_target_pairs={{0,7},{1,0},{2,1},{3,2},{4,3},{5,4},{6,5},{7,6},{8,15},{9,8},{10,9... | collective-permute-start | bytes 786440 | tf_op jit(solution)/shard_map/ppermute | solution.py:472
  95.5 41.5 %copy-start.6 = (bf16[256,512]{1,0:T(8,128)(2,1)}, bf16[256,512]{1,0:T(8,128)(2,1)S(1)}, u32[]{:S(2)}) copy-start(bf16[256,512]{1,0:T(8,128)(2,1)S(1)} %attend.3.refs_8_) | copy-start | bytes 786436
  96.1 9.0 %collective-permute-start.10 = (bf16[256,512]{1,0:T(8,128)(2,1)S(1)}, bf16[256,512]{1,0:T(8,128)(2,1)S(1)}, u32[]{:S(2)}, u32[]{:S(2)}) collective-permute-start(bf16[256,512]{1,0:T(8,128)(2,1)S(1)} %attend.3.refs_8_), channel_id=1, source_target_pairs={{0,7},{1,0},{2,1},{3,2},{4,3},{5,4},{6,5},{7,6},{8,15},{9,8},{10,9... | collective-permute-start | bytes 786440 | tf_op jit(solution)/shard_map/ppermute | solution.py:472
  99.1 10.4 %collective-permute-start.9 = (bf16[256,512]{1,0:T(8,128)(2,1)S(1)}, bf16[256,512]{1,0:T(8,128)(2,1)S(1)}, u32[]{:S(2)}, u32[]{:S(2)}) collective-permute-start(bf16[256,512]{1,0:T(8,128)(2,1)S(1)} %attend.3.refs_8_), channel_id=1, source_target_pairs={{0,1},{1,2},{2,3},{3,4},{4,5},{5,6},{6,7},{7,0},{8,9},{9,10},{10,1... | collective-permute-start | bytes 786440 | tf_op jit(solution)/shard_map/ppermute | solution.py:472
  99.1 16.0 %collective-permute-start.4 = (bf16[256,512]{1,0:T(8,128)(2,1)S(1)}, bf16[256,512]{1,0:T(8,128)(2,1)S(1)}, u32[]{:S(2)}, u32[]{:S(2)}) collective-permute-start(bf16[256,512]{1,0:T(8,128)(2,1)S(1)} %collective-permute-done.2.refs_1_), channel_id=1, source_target_pairs={{0,1},{1,2},{2,3},{3,4},{4,5},{5,6},{6,7},{7,0},{8,9},{9,10},{10,1... | collective-permute-start | bytes 786440 | tf_op jit(solution)/shard_map/ppermute | solution.py:472
  105.1 31.9 %copy-start.9 = (bf16[256,512]{1,0:T(8,128)(2,1)}, bf16[256,512]{1,0:T(8,128)(2,1)S(1)}, u32[]{:S(2)}) copy-start(bf16[256,512]{1,0:T(8,128)(2,1)S(1)} %collective-permute-done.10.refs_10_) | copy-start | bytes 786436
  105.1 10.5 %collective-permute-start.12 = (bf16[256,512]{1,0:T(8,128)(2,1)S(1)}, bf16[256,512]{1,0:T(8,128)(2,1)S(1)}, u32[]{:S(2)}, u32[]{:S(2)}) collective-permute-start(bf16[256,512]{1,0:T(8,128)(2,1)S(1)} %collective-permute-done.10.refs_10_), channel_id=1, source_target_pairs={{0,7},{1,0},{2,1},{3,2},{4,3},{5,4},{6,5},{7,6},{8,15},{9,8},{10,9... | collective-permute-start | bytes 786440 | tf_op jit(solution)/shard_map/ppermute | solution.py:472
  108.8 12.4 %collective-permute-start.5 = (bf16[256,512]{1,0:T(8,128)(2,1)S(1)}, bf16[256,512]{1,0:T(8,128)(2,1)S(1)}, u32[]{:S(2)}, u32[]{:S(2)}) collective-permute-start(bf16[256,512]{1,0:T(8,128)(2,1)S(1)} %collective-permute-done.3.refs_2_), channel_id=1, source_target_pairs={{0,7},{1,0},{2,1},{3,2},{4,3},{5,4},{6,5},{7,6},{8,15},{9,8},{10,9... | collective-permute-start | bytes 786440 | tf_op jit(solution)/shard_map/ppermute | solution.py:472
  109.5 27.5 %copy-start.10 = (bf16[256,512]{1,0:T(8,128)(2,1)}, bf16[256,512]{1,0:T(8,128)(2,1)S(1)}, u32[]{:S(2)}) copy-start(bf16[256,512]{1,0:T(8,128)(2,1)S(1)} %collective-permute-done.9.refs_9_) | copy-start | bytes 786436
  109.5 15.4 %collective-permute-start.11 = (bf16[256,512]{1,0:T(8,128)(2,1)S(1)}, bf16[256,512]{1,0:T(8,128)(2,1)S(1)}, u32[]{:S(2)}, u32[]{:S(2)}) collective-permute-start(bf16[256,512]{1,0:T(8,128)(2,1)S(1)} %collective-permute-done.9.refs_9_), channel_id=1, source_target_pairs={{0,1},{1,2},{2,3},{3,4},{4,5},{5,6},{6,7},{7,0},{8,9},{9,10},{10,1... | collective-permute-start | bytes 786440 | tf_op jit(solution)/shard_map/ppermute | solution.py:472
  115.1 10.3 %collective-permute-start.6 = (bf16[256,512]{1,0:T(8,128)(2,1)S(1)}, bf16[256,512]{1,0:T(8,128)(2,1)S(1)}, u32[]{:S(2)}, u32[]{:S(2)}) collective-permute-start(bf16[256,512]{1,0:T(8,128)(2,1)S(1)} %collective-permute-done.4.refs_3_), channel_id=1, source_target_pairs={{0,1},{1,2},{2,3},{3,4},{4,5},{5,6},{6,7},{7,0},{8,9},{9,10},{10,1... | collective-permute-start | bytes 786440 | tf_op jit(solution)/shard_map/ppermute | solution.py:472
  115.6 21.4 %copy-start.11 = (bf16[256,512]{1,0:T(8,128)(2,1)}, bf16[256,512]{1,0:T(8,128)(2,1)S(1)}, u32[]{:S(2)}) copy-start(bf16[256,512]{1,0:T(8,128)(2,1)S(1)} %collective-permute-done.12.refs_12_) | copy-start | bytes 786436
  115.6 11.2 %collective-permute-start.14 = (bf16[256,512]{1,0:T(8,128)(2,1)S(1)}, bf16[256,512]{1,0:T(8,128)(2,1)S(1)}, u32[]{:S(2)}, u32[]{:S(2)}) collective-permute-start(bf16[256,512]{1,0:T(8,128)(2,1)S(1)} %collective-permute-done.12.refs_12_), channel_id=1, source_target_pairs={{0,7},{1,0},{2,1},{3,2},{4,3},{5,4},{6,5},{7,6},{8,15},{9,8},{10,9... | collective-permute-start | bytes 786440 | tf_op jit(solution)/shard_map/ppermute | solution.py:472
  121.2 11.2 %collective-permute-start.7 = (bf16[256,512]{1,0:T(8,128)(2,1)S(1)}, bf16[256,512]{1,0:T(8,128)(2,1)S(1)}, u32[]{:S(2)}, u32[]{:S(2)}) collective-permute-start(bf16[256,512]{1,0:T(8,128)(2,1)S(1)} %collective-permute-done.5.refs_4_), channel_id=1, source_target_pairs={{0,7},{1,0},{2,1},{3,2},{4,3},{5,4},{6,5},{7,6},{8,15},{9,8},{10,9... | collective-permute-start | bytes 786440 | tf_op jit(solution)/shard_map/ppermute | solution.py:472
  124.9 12.1 %copy-start.12 = (bf16[256,512]{1,0:T(8,128)(2,1)}, bf16[256,512]{1,0:T(8,128)(2,1)S(1)}, u32[]{:S(2)}) copy-start(bf16[256,512]{1,0:T(8,128)(2,1)S(1)} %collective-permute-done.11.refs_11_) | copy-start | bytes 786436
  124.9 9.3 %collective-permute-start.13 = (bf16[256,512]{1,0:T(8,128)(2,1)S(1)}, bf16[256,512]{1,0:T(8,128)(2,1)}, u32[]{:S(2)}, u32[]{:S(2)}) collective-permute-start(bf16[256,512]{1,0:T(8,128)(2,1)S(1)} %collective-permute-done.11.refs_11_), channel_id=1, source_target_pairs={{0,1},{1,2},{2,3},{3,4},{4,5},{5,6},{6,7},{7,0},{8,9},{9,10},{10,1... | collective-permute-start | bytes 786440 | tf_op jit(solution)/shard_map/ppermute | solution.py:472
  125.4 11.6 %collective-permute-start.8 = (bf16[256,512]{1,0:T(8,128)(2,1)S(1)}, bf16[256,512]{1,0:T(8,128)(2,1)}, u32[]{:S(2)}, u32[]{:S(2)}) collective-permute-start(bf16[256,512]{1,0:T(8,128)(2,1)S(1)} %collective-permute-done.6.refs_5_), channel_id=1, source_target_pairs={{0,1},{1,2},{2,3},{3,4},{4,5},{5,6},{6,7},{7,0},{8,9},{9,10},{10,1... | collective-permute-start | bytes 786440 | tf_op jit(solution)/shard_map/ppermute | solution.py:472
  126.8 10.2 %copy-start.13 = (bf16[256,512]{1,0:T(8,128)(2,1)}, bf16[256,512]{1,0:T(8,128)(2,1)S(1)}, u32[]{:S(2)}) copy-start(bf16[256,512]{1,0:T(8,128)(2,1)S(1)} %collective-permute-done.14.refs_14_) | copy-start | bytes 786436
  126.8 10.2 %collective-permute-start.15 = (bf16[256,512]{1,0:T(8,128)(2,1)S(1)}, bf16[256,512]{1,0:T(8,128)(2,1)}, u32[]{:S(2)}, u32[]{:S(2)}) collective-permute-start(bf16[256,512]{1,0:T(8,128)(2,1)S(1)} %collective-permute-done.14.refs_14_), channel_id=1, source_target_pairs={{0,7},{1,0},{2,1},{3,2},{4,3},{5,4},{6,5},{7,6},{8,15},{9,8},{10,9... | collective-permute-start | bytes 786440 | tf_op jit(solution)/shard_map/ppermute | solution.py:472
Sparse Core Ops, SparseCore 0:
  72.5 64.4 all-gather.2
